TPU v7x, 32 devices: a whole 2x2x4 slice. The times are simulated.
32 devices in a mesh: dp: 2 (over x), ctx: 4 (over y, core), tp: 4 (over z).
Axes of the slice: x: 2, y: 2, z: 4, core: 2. Of those that a mesh axis runs over, the one named last changes fastest.
Arguments:
- tokens: bfloat16 [8192, 768], P(('dp', 'ctx')), may hold values from -6 to 6
- w_query: bfloat16 [768, 768], P('dp', 'tp'), may hold values from -0.3125 to 0.3125
- w_key: bfloat16 [768, 768], P('dp', 'tp'), may hold values from -0.3125 to 0.3125
- w_value: bfloat16 [768, 768], P('dp', 'tp'), may hold values from -0.21875 to 0.21875
- w_out: bfloat16 [768, 768], P('tp', 'dp'), may hold values from -1.75 to 1.75
- w_act: bfloat16 [768, 1152], P('dp', 'tp'), may hold values from -0.21875 to 0.21875
- w_up: bfloat16 [768, 1152], P('dp', 'tp'), may hold values from -0.21875 to 0.21875
- w_down: bfloat16 [1152, 768], P('tp', 'dp'), may hold values from -0.1875 to 0.1875
- gain_one: bfloat16 [768], P('dp'), may hold values from 0.5 to 1.5
- gain_two: bfloat16 [768], P('dp'), may hold values from 0.5 to 1.5
- cotangent: bfloat16 [8192, 768], P(('dp', 'ctx')), may hold values from -6 to 6
Outputs:
- outputs: bfloat16 [8192, 768], P(('dp', 'ctx', 'tp'))
- input_grad: bfloat16 [8192, 768], P(('dp', 'ctx', 'tp'))
- grad_query: float32 [768, 768], P('dp', 'tp')
- grad_key: float32 [768, 768], P('dp', 'tp')
- grad_value: float32 [768, 768], P('dp', 'tp')
- grad_out: float32 [768, 768], P('tp', 'dp')
- grad_act: float32 [768, 1152], P('dp', 'tp')
- grad_up: float32 [768, 1152], P('dp', 'tp')
- grad_down: float32 [1152, 768], P('tp', 'dp')
- grad_gain_one: float32 [768], P('dp')
- grad_gain_two: float32 [768], P('dp')
All inputs are finite; a program needn't handle non-finite values.
Results may differ from a plain program's by a relative error of at most 0.024.
Values may be sent and summed in bfloat16 or wider, within the bound.
A program may use at most 128 MiB of HBM per device.

v0:
```python
import math

import jax
import jax.numpy as jnp
from jax import lax
from jax.sharding import PartitionSpec as P

HEAD = 64


EPSILON = 1e-05
ROPE_BASE = 160000.0


def standardize(values_in):
    mean_value = jnp.mean(values_in, axis=-1, keepdims=True)
    centred = values_in - mean_value
    inverse = lax.rsqrt(jnp.mean(centred * centred, axis=-1, keepdims=True) + EPSILON)
    return (centred * inverse, inverse)


def norm_back(grad_hat, hat_values, inverse):
    mean_grad = jnp.mean(grad_hat, axis=-1, keepdims=True)
    mean_cross = jnp.mean(grad_hat * hat_values, axis=-1, keepdims=True)
    return inverse * (grad_hat - mean_grad - hat_values * mean_cross)


def rotate(tensor):
    half_size = tensor.shape[-1] // 2
    return jnp.concatenate([-tensor[..., half_size:], tensor[..., :half_size]], axis=-1)


def unrotate(tensor):
    half_size = tensor.shape[-1] // 2
    return jnp.concatenate([tensor[..., half_size:], -tensor[..., :half_size]], axis=-1)


def rotary(tensor, cosine_table, sine_table):
    return tensor * cosine_table + rotate(tensor) * sine_table


def rotary_back(tensor, cosine_table, sine_table):
    return tensor * cosine_table + unrotate(tensor * sine_table)


def tables(offset, length, head_size):
    position = (offset + jnp.arange(length)).astype(jnp.float32)
    frequency = ROPE_BASE ** (-jnp.arange(0, head_size, 2).astype(jnp.float32) / head_size)
    angles = position[:, None] * frequency[None, :]
    angles = jnp.concatenate([angles, angles], axis=1)
    return (jnp.cos(angles)[:, None, :], jnp.sin(angles)[:, None, :])


def gelu_parts(values_in):
    normal_cdf = 0.5 * (1.0 + lax.erf(values_in * (1.0 / math.sqrt(2.0))))
    density = jnp.exp(-0.5 * values_in * values_in) * (1.0 / math.sqrt(2.0 * math.pi))
    return (values_in * normal_cdf, normal_cdf + values_in * density)


def block_scores(query_block, key_block, factor):
    return (
        jnp.einsum("qhd,khd->hqk", query_block, key_block, preferred_element_type=jnp.float32)
        * factor
    )


def attend(queries, key_data, value_data, head_count):
    query_rows = queries.shape[0]
    key_rows = key_data.shape[0]
    query_step = math.gcd(query_rows, 512)
    factor = HEAD ** (-0.5)
    query_blocks = queries.reshape(query_rows // query_step, query_step, head_count, HEAD)
    key_all = key_data.reshape(key_rows, head_count, HEAD)
    value_all = value_data.reshape(key_rows, head_count, HEAD)

    def per_query(query_block):
        scores = block_scores(query_block, key_all, factor)
        log_total = jax.nn.logsumexp(scores, axis=-1)
        weights = jnp.exp(scores - log_total[:, :, None]).astype(jnp.bfloat16)
        accumulated = jnp.einsum(
            "hqk,khd->qhd", weights, value_all, preferred_element_type=jnp.float32
        )
        return (accumulated.reshape(query_step, head_count * HEAD), log_total.T)

    mixed_blocks, log_blocks = lax.map(per_query, query_blocks)
    return (
        mixed_blocks.reshape(query_rows, head_count * HEAD),
        log_blocks.reshape(query_rows, head_count),
    )


def attend_back(queries, grad_mixed, log_totals, totals, key_data, value_data, head_count):
    query_rows = queries.shape[0]
    key_rows = key_data.shape[0]
    query_step = math.gcd(query_rows, 512)
    key_step = math.gcd(key_rows, 1024)
    factor = HEAD ** (-0.5)
    query_blocks = queries.reshape(query_rows // query_step, query_step, head_count, HEAD)
    grad_blocks = grad_mixed.reshape(query_rows // query_step, query_step, head_count, HEAD)
    log_blocks = log_totals.reshape(query_rows // query_step, query_step, head_count)
    total_blocks = totals.reshape(query_rows // query_step, query_step, head_count)
    key_blocks = key_data.reshape(key_rows // key_step, key_step, head_count, HEAD)
    value_blocks = value_data.reshape(key_rows // key_step, key_step, head_count, HEAD)

    def per_query(running, block_item):
        key_accum, value_accum = running
        query_block, grad_block, log_block, total_block = block_item

        def per_key(query_accum, key_item):
            key_block, value_block, key_sum, value_sum = key_item
            scores = block_scores(query_block, key_block, factor)
            weights_full = jnp.exp(scores - log_block.T[:, :, None])
            value_sum = value_sum + jnp.einsum(
                "hqk,qhd->khd",
                weights_full.astype(jnp.bfloat16),
                grad_block,
                preferred_element_type=jnp.float32,
            )
            grad_probs = jnp.einsum(
                "qhd,khd->hqk", grad_block, value_block, preferred_element_type=jnp.float32
            )
            grad_scores = (factor * weights_full * (grad_probs - total_block.T[:, :, None])).astype(
                jnp.bfloat16
            )
            query_accum = query_accum + jnp.einsum(
                "hqk,khd->qhd", grad_scores, key_block, preferred_element_type=jnp.float32
            )
            key_sum = key_sum + jnp.einsum(
                "hqk,qhd->khd", grad_scores, query_block, preferred_element_type=jnp.float32
            )
            return (query_accum, (key_sum, value_sum))

        initial = jnp.zeros((query_step, head_count, HEAD), jnp.float32)
        query_accum, (key_accum, value_accum) = lax.scan(
            per_key, initial, (key_blocks, value_blocks, key_accum, value_accum)
        )
        return ((key_accum, value_accum), query_accum)

    zero_blocks = jnp.zeros(key_blocks.shape, jnp.float32)
    (key_accum, value_accum), query_accum = lax.scan(
        per_query, (zero_blocks, zero_blocks), (query_blocks, grad_blocks, log_blocks, total_blocks)
    )
    feature_count = head_count * HEAD
    return (
        query_accum.reshape(query_rows, feature_count),
        key_accum.reshape(key_rows, feature_count),
        value_accum.reshape(key_rows, feature_count),
    )


def owner_shares(
    query_grad,
    key_grad,
    value_grad,
    act_grad,
    up_grad,
    gain_first_grad,
    gain_second_grad,
    out_grad,
    down_grad,
):
    row_parts = (
        lax.psum_scatter(
            query_grad.astype(jnp.bfloat16), "dp", scatter_dimension=0, tiled=True
        ).astype(jnp.float32),
        lax.psum_scatter(
            key_grad.astype(jnp.bfloat16), "dp", scatter_dimension=0, tiled=True
        ).astype(jnp.float32),
        lax.psum_scatter(
            value_grad.astype(jnp.bfloat16), "dp", scatter_dimension=0, tiled=True
        ).astype(jnp.float32),
        lax.psum_scatter(
            act_grad.astype(jnp.bfloat16), "dp", scatter_dimension=0, tiled=True
        ).astype(jnp.float32),
        lax.psum_scatter(
            up_grad.astype(jnp.bfloat16), "dp", scatter_dimension=0, tiled=True
        ).astype(jnp.float32),
        lax.psum_scatter(
            gain_first_grad.astype(jnp.bfloat16), "dp", scatter_dimension=0, tiled=True
        ).astype(jnp.float32),
        lax.psum_scatter(
            gain_second_grad.astype(jnp.bfloat16), "dp", scatter_dimension=0, tiled=True
        ).astype(jnp.float32),
    )
    col_parts = (
        lax.psum_scatter(
            out_grad.astype(jnp.bfloat16), "dp", scatter_dimension=1, tiled=True
        ).astype(jnp.float32),
        lax.psum_scatter(
            down_grad.astype(jnp.bfloat16), "dp", scatter_dimension=1, tiled=True
        ).astype(jnp.float32),
    )
    return tuple(row_parts) + tuple(col_parts)


def context_total(query_grad, key_grad, value_grad, act_grad, up_grad, out_grad, down_grad):
    return tuple(
        (
            lax.psum(query_grad.astype(jnp.bfloat16), "ctx").astype(jnp.float32),
            lax.psum(key_grad.astype(jnp.bfloat16), "ctx").astype(jnp.float32),
            lax.psum(value_grad.astype(jnp.bfloat16), "ctx").astype(jnp.float32),
            lax.psum(act_grad.astype(jnp.bfloat16), "ctx").astype(jnp.float32),
            lax.psum(up_grad.astype(jnp.bfloat16), "ctx").astype(jnp.float32),
            lax.psum(out_grad.astype(jnp.bfloat16), "ctx").astype(jnp.float32),
            lax.psum(down_grad.astype(jnp.bfloat16), "ctx").astype(jnp.float32),
        )
    )


def local(
    tokens, w_query, w_key, w_value, w_out, w_act, w_up, w_down, gain_one, gain_two, cotangent
):
    tok_rows = tokens.shape[0]
    query_w, key_w, value_w, act_w, up_w, gain_first, gain_second = (
        lax.all_gather(w_query, "dp", axis=0, tiled=True),
        lax.all_gather(w_key, "dp", axis=0, tiled=True),
        lax.all_gather(w_value, "dp", axis=0, tiled=True),
        lax.all_gather(w_act, "dp", axis=0, tiled=True),
        lax.all_gather(w_up, "dp", axis=0, tiled=True),
        lax.all_gather(gain_one, "dp", axis=0, tiled=True),
        lax.all_gather(gain_two, "dp", axis=0, tiled=True),
    )
    out_w, down_w = (
        lax.all_gather(w_out, "dp", axis=1, tiled=True),
        lax.all_gather(w_down, "dp", axis=1, tiled=True),
    )
    head_count = query_w.shape[1] // HEAD
    feature_count = head_count * HEAD
    share_rows = tok_rows // lax.axis_size("tp")
    share_start = lax.axis_index("tp") * share_rows

    def own_rows(array_in):
        return lax.dynamic_slice_in_dim(array_in, share_start, share_rows, 0)

    cosine_table, sine_table = tables(lax.axis_index("ctx") * tok_rows, tok_rows, HEAD)
    gain_first_f = gain_first.astype(jnp.float32)
    gain_second_f = gain_second.astype(jnp.float32)
    inputs = tokens.astype(jnp.float32)
    hat_one, inverse_one = standardize(inputs)
    normed = (hat_one * gain_first_f).astype(jnp.bfloat16)
    query_pre = jnp.dot(normed, query_w, preferred_element_type=jnp.float32).reshape(
        tok_rows, head_count, HEAD
    )
    key_pre = jnp.dot(normed, key_w, preferred_element_type=jnp.float32).reshape(
        tok_rows, head_count, HEAD
    )
    queries = (
        rotary(query_pre, cosine_table, sine_table)
        .astype(jnp.bfloat16)
        .reshape(tok_rows, feature_count)
    )
    key_data = (
        rotary(key_pre, cosine_table, sine_table)
        .astype(jnp.bfloat16)
        .reshape(tok_rows, feature_count)
    )
    value_data = jnp.dot(normed, value_w, preferred_element_type=jnp.float32).astype(jnp.bfloat16)
    keys_all, values_all = (
        lax.all_gather(key_data, "ctx", axis=0, tiled=True),
        lax.all_gather(value_data, "ctx", axis=0, tiled=True),
    )
    mixed_full, log_totals = attend(
        queries.reshape(tok_rows, head_count, HEAD), keys_all, values_all, head_count
    )
    mixed_low = mixed_full.astype(jnp.bfloat16)
    middle = inputs + lax.psum(
        jnp.dot(mixed_low, out_w, preferred_element_type=jnp.float32).astype(jnp.bfloat16), "tp"
    ).astype(jnp.float32)
    hat_two, inverse_two = standardize(middle)
    normed_two = (hat_two * gain_second_f).astype(jnp.bfloat16)
    gate_in = jnp.dot(normed_two, act_w, preferred_element_type=jnp.float32)
    up_in = jnp.dot(normed_two, up_w, preferred_element_type=jnp.float32)
    active_in, derivative_in = gelu_parts(gate_in)
    hidden = (active_in * up_in).astype(jnp.bfloat16)
    outputs = middle + lax.psum(
        jnp.dot(hidden, down_w, preferred_element_type=jnp.float32).astype(jnp.bfloat16), "tp"
    ).astype(jnp.float32)
    out_rows = own_rows(outputs)
    grad_hidden = jnp.dot(cotangent, down_w.T, preferred_element_type=jnp.float32)
    grad_gate = (grad_hidden * up_in * derivative_in).astype(jnp.bfloat16)
    grad_upin = (grad_hidden * active_in).astype(jnp.bfloat16)
    down_grad = jnp.dot(hidden.T, cotangent, preferred_element_type=jnp.float32)
    act_grad = jnp.dot(normed_two.T, grad_gate, preferred_element_type=jnp.float32)
    up_grad = jnp.dot(normed_two.T, grad_upin, preferred_element_type=jnp.float32)
    grad_normed_two = lax.psum(
        (
            jnp.dot(grad_gate, act_w.T, preferred_element_type=jnp.float32)
            + jnp.dot(grad_upin, up_w.T, preferred_element_type=jnp.float32)
        ).astype(jnp.bfloat16),
        "tp",
    ).astype(jnp.float32)
    gain_second_grad = jnp.sum(own_rows(grad_normed_two) * own_rows(hat_two), axis=0)
    grad_middle = cotangent.astype(jnp.float32) + norm_back(
        grad_normed_two * gain_second_f, hat_two, inverse_two
    )
    grad_middle_low = grad_middle.astype(jnp.bfloat16)
    grad_middle_part = own_rows(grad_middle)
    out_grad = jnp.dot(mixed_low.T, grad_middle_low, preferred_element_type=jnp.float32)
    grad_mixed = jnp.dot(grad_middle_low, out_w.T, preferred_element_type=jnp.float32).astype(
        jnp.bfloat16
    )
    totals = jnp.sum(
        (grad_mixed.astype(jnp.float32) * mixed_full).reshape(tok_rows, head_count, HEAD), axis=-1
    )
    grad_qrot, key_part, value_part = attend_back(
        queries, grad_mixed, log_totals, totals, keys_all, values_all, head_count
    )
    grad_krot, grad_values = (
        lax.psum_scatter(
            key_part.astype(jnp.bfloat16), "ctx", scatter_dimension=0, tiled=True
        ).astype(jnp.float32),
        lax.psum_scatter(
            value_part.astype(jnp.bfloat16), "ctx", scatter_dimension=0, tiled=True
        ).astype(jnp.float32),
    )
    grad_q = (
        rotary_back(grad_qrot.reshape(tok_rows, head_count, HEAD), cosine_table, sine_table)
        .reshape(tok_rows, feature_count)
        .astype(jnp.bfloat16)
    )
    grad_k = (
        rotary_back(grad_krot.reshape(tok_rows, head_count, HEAD), cosine_table, sine_table)
        .reshape(tok_rows, feature_count)
        .astype(jnp.bfloat16)
    )
    grad_v = grad_values.astype(jnp.bfloat16)
    query_grad = jnp.dot(normed.T, grad_q, preferred_element_type=jnp.float32)
    key_grad = jnp.dot(normed.T, grad_k, preferred_element_type=jnp.float32)
    value_grad = jnp.dot(normed.T, grad_v, preferred_element_type=jnp.float32)
    grad_normed_part = own_rows(
        lax.psum(
            (
                jnp.dot(grad_q, query_w.T, preferred_element_type=jnp.float32)
                + jnp.dot(grad_k, key_w.T, preferred_element_type=jnp.float32)
                + jnp.dot(grad_v, value_w.T, preferred_element_type=jnp.float32)
            ).astype(jnp.bfloat16),
            "tp",
        ).astype(jnp.float32)
    )
    hat_one_part = own_rows(hat_one)
    gain_first_part = jnp.sum(grad_normed_part * hat_one_part, axis=0)
    input_rows = grad_middle_part + norm_back(
        grad_normed_part * gain_first_f, hat_one_part, own_rows(inverse_one)
    )
    gain_first_grad, gain_second_total = lax.psum(
        (gain_first_part, gain_second_grad), ("ctx", "tp")
    )
    summed = context_total(query_grad, key_grad, value_grad, act_grad, up_grad, out_grad, down_grad)
    shares = owner_shares(
        summed[0],
        summed[1],
        summed[2],
        summed[3],
        summed[4],
        gain_first_grad,
        gain_second_total,
        summed[5],
        summed[6],
    )
    return (
        out_rows.astype(jnp.bfloat16),
        input_rows.astype(jnp.bfloat16),
        shares[0],
        shares[1],
        shares[2],
        shares[7],
        shares[3],
        shares[4],
        shares[8],
        shares[5],
        shares[6],
    )


def solution(mesh):
    in_specs = (
        P(("dp", "ctx"), None),
        P("dp", "tp"),
        P("dp", "tp"),
        P("dp", "tp"),
        P("tp", "dp"),
        P("dp", "tp"),
        P("dp", "tp"),
        P("tp", "dp"),
        P("dp"),
        P("dp"),
        P(("dp", "ctx"), None),
    )
    out_specs = (
        P(("dp", "ctx", "tp"), None),
        P(("dp", "ctx", "tp"), None),
        P("dp", "tp"),
        P("dp", "tp"),
        P("dp", "tp"),
        P("tp", "dp"),
        P("dp", "tp"),
        P("dp", "tp"),
        P("tp", "dp"),
        P("dp"),
        P("dp"),
    )
    return jax.shard_map(local, mesh=mesh, in_specs=in_specs, out_specs=out_specs, check_vma=False)
```

profile of v0, /device:TPU:0, one launch (start us, length us, event | category | flops | bytes accessed | tf_op | source)
XLA Modules:
  0.0 796.8 jit_solution(9328104708917841218)
XLA Ops:
  8.1 5.2 all-gather
  17.1 5.8 all_gather.37
  26.6 5.8 all_gather.35
  35.4 5.8 all_gather.34
  48.6 6.1 all_gather.39
  54.7 15.3 %all-gather.5.cloned.1.call-done = bf16[4096,192]{0,1:T(8,128)(2,1)} async-done(((bf16[1024,192]{0,1:T(8,128)(2,1)}), bf16[4096,192]{0,1:T(8,128)(2,1)}) %all-gather.5.cloned.1.call-update) | async-done | bytes 1572880 | tf_op jit(solution)/shard_map/all_gather | solution.py:259
  69.9 58.7 %while.42 = (s32[]{:T(128)}, f32[2,512,192]{1,0,2:T(2,128)}, f32[2,512,3]{1,2,0:T(4,128)S(1)}, bf16[2,512,3,64]{1,3,2,0:T(8,128)(2,1)S(1)}, bf16[4096,3,64]{0,2,...) while((s32[]{:T(128)}, f32[2,512,192]{1,0,2:T(2,128)}, f32[2,512,3]{1,2,0:T(4,128)S(1)}, ...), condition=%wide.region_5.6_spmd, body=%wide.region_2.5_spmd.sunk | while | flops 1660956672 | bytes 194132176 | solution.py:85
  74.9 5.0 exponential_reduce_fusion.2
  83.8 10.6 %fusion.155 = f32[3,512,64]{1,2,0:T(8,128)S(1)} fusion(bf16[4096,3,64]{0,2,1:T(8,128)(2,1)S(1)} %copy-done.2, f32[3,512,4096]{2,1,0:T(8,128)} %copy-done, f32[3,512]{1,0:T(4,128)S(1)} %fusion.154), kind=kOutput, calls=%fused_computation.3.clone.1 | convolution fusion | flops 824180736 | bytes 27138048 | tf_op jit(solution)/shard_map/while/body/eval_jaxpr/hqk,khd->qhd/dot_general | solution.py:80
  99.3 5.0 multiply_reduce_fusion.6
  113.1 10.6 %fusion.155 = f32[3,512,64]{1,2,0:T(8,128)S(1)} fusion(bf16[4096,3,64]{0,2,1:T(8,128)(2,1)S(1)} %copy-done.2, f32[3,512,4096]{2,1,0:T(8,128)} %copy-done, f32[3,512]{1,0:T(4,128)S(1)} %fusion.154), kind=kOutput, calls=%fused_computation.3.clone.1 | convolution fusion | flops 824180736 | bytes 27138048 | tf_op jit(solution)/shard_map/while/body/eval_jaxpr/hqk,khd->qhd/dot_general | solution.py:80
  138.1 7.2 all_gather.41
  145.3 6.7 all_gather.42
  152.0 6.9 all_gather.43
  158.9 43.4 %all-reduce.11.cloned.1.call-done = bf16[1024,768]{1,0:T(8,128)(2,1)} async-done(((bf16[1024,768]{1,0:T(8,128)(2,1)}), bf16[1024,768]{1,0:T(8,128)(2,1)}) %all-reduce.11.cloned.1.call-update) | async-done | bytes 1572880 | tf_op jit(solution)/shard_map/psum | solution.py:266
  226.1 58.2 %all-reduce.13.cloned.1.call-done = bf16[1024,768]{1,0:T(8,128)(2,1)} async-done(((bf16[1024,768]{1,0:T(8,128)(2,1)}), bf16[1024,768]{1,0:T(8,128)(2,1)}) %all-reduce.13.cloned.1.call-update) | async-done | bytes 1572880 | tf_op jit(solution)/shard_map/psum | solution.py:285
  299.2 99.6 %while.44 = (s32[]{:T(128)}, f32[4,1024,3,64]{1,3,2,0:T(8,128)}, f32[4,1024,3,64]{1,3,2,0:T(8,128)}, f32[2,512,3,64]{1,0,3,2:T(2,128)}, bf16[2,512,3,64]{1,3,2,0...) while((s32[]{:T(128)}, f32[4,1024,3,64]{1,3,2,0:T(8,128)}, ...), condition=%wide.region_17.18_spmd, body=%wide.region_14.17_spmd.sunk | while | flops 1021378560 | bytes 39758236 | solution.py:140
  299.3 41.3 %while.45 = (s32[]{:T(128)}, f32[512,3,64]{0,2,1:T(8,128)S(1)}, f32[4,1024,3,64]{1,3,2,0:T(8,128)}, f32[4,1024,3,64]{1,3,2,0:T(8,128)}, bf16[4,1024,3,64]{1,3,2,...) while((s32[]{:T(128)}, f32[512,3,64]{0,2,1:T(8,128)S(1)}, ...), condition=%wide.region_16.16_spmd.clone.clone, body=%wide.region_15.15_spmd.clone.clone.sunk | while | flops 1021378560 | bytes 37374108 | solution.py:134
  341.0 8.1 %dynamic_update_slice.33 = f32[2,512,3,64]{1,0,3,2:T(2,128)} dynamic-update-slice(f32[2,512,3,64]{1,0,3,2:T(2,128)} %get-tuple-element.656, f32[1,512,3,64]{1,0,3,2:T(1,128)S(1)} %copy.87, s32[]{:T(128)S(6)} %copy.120, s32[]{:T(128)} %constant.57.clone.1..sunk.1, s32[]{:T(128)} %constant.57.clone.1..sunk.1, s32[]{:T(128)} %constant.57.clone.1..sunk.1) | dynamic-update-slice | bytes 786436 | tf_op jit(solution)/shard_map/while/body/jit(dynamic_update_index_in_dim)/dynamic_update_slice | solution.py:140
  349.1 41.3 %while.45 = (s32[]{:T(128)}, f32[512,3,64]{0,2,1:T(8,128)S(1)}, f32[4,1024,3,64]{1,3,2,0:T(8,128)}, f32[4,1024,3,64]{1,3,2,0:T(8,128)}, bf16[4,1024,3,64]{1,3,2,...) while((s32[]{:T(128)}, f32[512,3,64]{0,2,1:T(8,128)S(1)}, ...), condition=%wide.region_16.16_spmd.clone.clone, body=%wide.region_15.15_spmd.clone.clone.sunk | while | flops 1021378560 | bytes 37374108 | solution.py:134
  390.8 8.1 %dynamic_update_slice.33 = f32[2,512,3,64]{1,0,3,2:T(2,128)} dynamic-update-slice(f32[2,512,3,64]{1,0,3,2:T(2,128)} %get-tuple-element.656, f32[1,512,3,64]{1,0,3,2:T(1,128)S(1)} %copy.87, s32[]{:T(128)S(6)} %copy.120, s32[]{:T(128)} %constant.57.clone.1..sunk.1, s32[]{:T(128)} %constant.57.clone.1..sunk.1, s32[]{:T(128)} %constant.57.clone.1..sunk.1) | dynamic-update-slice | bytes 786436 | tf_op jit(solution)/shard_map/while/body/jit(dynamic_update_index_in_dim)/dynamic_update_slice | solution.py:140
  437.3 24.9 %reduce-scatter.26.cloned.1.call-done = bf16[1024,192]{0,1:T(8,128)(2,1)} async-done(((bf16[4096,192]{0,1:T(8,128)(2,1)}), bf16[1024,192]{0,1:T(8,128)(2,1)}) %reduce-scatter.26.cloned.1.call-update) | async-done | bytes 393232 | tf_op jit(solution)/shard_map/reduce_scatter | solution.py:312
  467.9 11.8 %reduce-scatter.40.cloned.1.call-done = bf16[384,288]{1,0:T(8,128)(2,1)} async-done(((bf16[768,288]{1,0:T(8,128)(2,1)}), bf16[384,288]{1,0:T(8,128)(2,1)}) %reduce-scatter.40.cloned.1.call-update) | async-done | bytes 221200
  481.6 15.9 %reduce-scatter.36.cloned.1.call-done = bf16[384,288]{1,0:T(8,128)(2,1)} async-done(((bf16[768,288]{1,0:T(8,128)(2,1)}), bf16[384,288]{1,0:T(8,128)(2,1)}) %reduce-scatter.36.cloned.1.call-update) | async-done | bytes 221200
  499.3 15.8 %reduce-scatter.38.cloned.1.call-done = bf16[384,288]{1,0:T(8,128)(2,1)} async-done(((bf16[768,288]{1,0:T(8,128)(2,1)}), bf16[384,288]{1,0:T(8,128)(2,1)}) %reduce-scatter.38.cloned.1.call-update) | async-done | bytes 221200
  516.8 14.1 %reduce-scatter.34.cloned.1.call-done = bf16[384,192]{1,0:T(8,128)(2,1)} async-done(((bf16[768,192]{1,0:T(8,128)(2,1)}), bf16[384,192]{1,0:T(8,128)(2,1)}) %reduce-scatter.34.cloned.1.call-update) | async-done | bytes 147472
  534.3 12.6 %reduce-scatter.30.cloned.1.call-done = bf16[384,192]{1,0:T(8,128)(2,1)} async-done(((bf16[768,192]{1,0:T(8,128)(2,1)}), bf16[384,192]{1,0:T(8,128)(2,1)}) %reduce-scatter.30.cloned.1.call-update) | async-done | bytes 147472
  548.6 14.2 %reduce-scatter.28.cloned.1.call-done = bf16[384,192]{1,0:T(8,128)(2,1)} async-done(((bf16[768,192]{1,0:T(8,128)(2,1)}), bf16[384,192]{1,0:T(8,128)(2,1)}) %reduce-scatter.28.cloned.1.call-update) | async-done | bytes 147472
  564.5 14.3 %reduce-scatter.32.cloned.1.call-done = bf16[384,192]{1,0:T(8,128)(2,1)} async-done(((bf16[768,192]{1,0:T(8,128)(2,1)}), bf16[384,192]{1,0:T(8,128)(2,1)}) %reduce-scatter.32.cloned.1.call-update) | async-done | bytes 147472
  588.4 33.7 %all-reduce.17.cloned.1.call-done = (bf16[384,192]{0,1:T(8,128)(2,1)}, bf16[384,192]{0,1:T(8,128)(2,1)}, bf16[384,192]{0,1:T(8,128)(2,1)}, bf16[192,384]{1,0:T(8...) async-done(((bf16[384,192]{0,1:T(8,128)(2,1)}, bf16[384,192]{0,1:T(8,128)(2,1)}, bf16[384,192]{0,1:T(8,128)(2,1)}, ...) | async-done | bytes 1253392 | tf_op jit(solution)/shard_map/psum | solution.py:199
  633.0 112.9 %all-reduce.15.cloned.1.call-done = (bf16[1024,768]{1,0:T(8,128)(2,1)}, bf16[1024,768]{1,0:T(8,128)(2,1)}) async-done(((bf16[1024,768]{1,0:T(8,128)(2,1)}, bf16[1024,768]{1,0:T(8,128)(2,1)}), (bf16[1024,768]{1,0:T(8,128)(2,1)}, bf16[1024,768]{1,0:T(8,128)(2,1)})) %all-reduce.15.cloned.1.call-update) | async-done | bytes 3145744 | tf_op jit(solution)/shard_map/psum | solution.py:275
  747.2 32.3 %all-reduce.2 = (bf16[768]{0:T(1024)(128)(2,1)S(1)}, bf16[768]{0:T(1024)(128)(2,1)S(1)}) all-reduce(f32[768]{0:T(1024)S(1)} %get-tuple-element.271, f32[768]{0:T(1024)S(1)} %multiply_reduce_fusion.4), channel_id=1, replica_groups=mesh['dp'=2,'ctx'=4,'tp'=4] {'ctx','tp'}, use_global_device_ids=true, to_apply=%region_38.39 | all-reduce | flops 1536 | bytes 9216 | tf_op jit(solution)/shard_map/psum | solution.py:345
  (343 shorter events, 264.5 us)
Async XLA Ops:
  7.2 15.7 %copy-start.4 = (bf16[1024,768]{1,0:T(8,128)(2,1)S(1)}, bf16[1024,768]{1,0:T(8,128)(2,1)}, u32[]{:S(2)}) copy-start(bf16[1024,768]{1,0:T(8,128)(2,1)} %param.17) | copy-start | bytes 4718596
  7.2 9.8 %copy-start.46 = (bf16[384,192]{0,1:T(8,128)(2,1)S(1)}, bf16[384,192]{0,1:T(8,128)(2,1)}, u32[]{:S(2)}) copy-start(bf16[384,192]{0,1:T(8,128)(2,1)} %param.20) | copy-start | bytes 442372
  7.2 47.5 %all-gather.7.cloned.1.call-start = ((), (), s32[]{:S(2)}) async-start(), calls=%async_computation.10 | async-start | bytes 1966080 | tf_op jit(solution)/shard_map/all_gather | solution.py:260
  13.3 11.8 %copy-start.50 = (f32[768]{0:T(1024)}, f32[768]{0:T(1024)S(1)}, u32[]{:S(2)}) copy-start(f32[768]{0:T(1024)S(1)} %reshape.248) | copy-start | bytes 9220
  25.1 16.1 %copy-start.6 = (bf16[1024,768]{1,0:T(8,128)(2,1)}, bf16[1024,768]{1,0:T(8,128)(2,1)S(1)}, u32[]{:S(2)}) copy-start(bf16[1024,768]{1,0:T(8,128)(2,1)S(1)} %get-tuple-element.356) | copy-start | bytes 4718596
  26.5 43.4 %all-gather.5.cloned.1.call-start = ((), (), s32[]{:S(2)}) async-start(), calls=%async_computation.9 | async-start | bytes 1966080 | tf_op jit(solution)/shard_map/all_gather | solution.py:259
  35.3 167.1 %all-reduce.11.cloned.1.call-start = ((), (), s32[]{:S(2)}) async-start(), calls=%async_computation.11 | async-start | bytes 3145728 | tf_op jit(solution)/shard_map/psum | solution.py:266
  74.9 8.9 %copy-start = (f32[3,512,4096]{2,1,0:T(8,128)}, f32[3,512,4096]{2,1,0:T(8,128)S(1)}, u32[]{:S(2)}) copy-start(f32[3,512,4096]{2,1,0:T(8,128)S(1)} %get-tuple-element.547) | copy-start | bytes 75497472 | tf_op jit(solution)/shard_map/while
  83.8 11.1 %copy-start.36 = (f32[2,512,192]{1,0,2:T(2,128)S(1)}, f32[2,512,192]{1,0,2:T(2,128)}, u32[]{:S(2)}) copy-start(f32[2,512,192]{1,0,2:T(2,128)} %get-tuple-element.624) | copy-start | bytes 2359300 | tf_op jit(solution)/shard_map/while
  113.1 11.0 %copy-start.36 = (f32[2,512,192]{1,0,2:T(2,128)S(1)}, f32[2,512,192]{1,0,2:T(2,128)}, u32[]{:S(2)}) copy-start(f32[2,512,192]{1,0,2:T(2,128)} %get-tuple-element.624) | copy-start | bytes 2359300 | tf_op jit(solution)/shard_map/while
  128.6 9.5 %copy-start.42 = (bf16[384,288]{0,1:T(8,128)(2,1)S(1)}, bf16[384,288]{0,1:T(8,128)(2,1)}, u32[]{:S(2)}) copy-start(bf16[384,288]{0,1:T(8,128)(2,1)} %param.22) | copy-start | bytes 663556
  128.6 16.7 %copy-start.43 = (bf16[384,288]{0,1:T(8,128)(2,1)S(1)}, bf16[384,288]{0,1:T(8,128)(2,1)}, u32[]{:S(2)}) copy-start(bf16[384,288]{0,1:T(8,128)(2,1)} %param.23) | copy-start | bytes 663556
  129.9 74.4 %copy-start.17 = (f32[24,8,2,512]{3,1,2,0:T(8,128)}, f32[24,8,2,512]{3,1,2,0:T(8,128)S(1)}, u32[]{:S(2)}) copy-start(f32[24,8,2,512]{3,1,2,0:T(8,128)S(1)} %copy.80) | copy-start | bytes 2359300
  130.0 22.1 %copy-start.44 = (bf16[288,384]{1,0:T(8,128)(2,1)S(1)}, bf16[288,384]{1,0:T(8,128)(2,1)}, u32[]{:S(2)}) copy-start(bf16[288,384]{1,0:T(8,128)(2,1)} %param.24) | copy-start | bytes 663556
  130.0 72.4 %copy-start.5 = (bf16[1024,768]{1,0:T(8,128)(2,1)S(1)}, bf16[1024,768]{1,0:T(8,128)(2,1)}, u32[]{:S(2)}) copy-start(bf16[1024,768]{1,0:T(8,128)(2,1)} %param.17) | copy-start | bytes 4718596
  133.1 151.2 %all-reduce.13.cloned.1.call-start = ((), (), s32[]{:S(2)}) async-start(), calls=%async_computation.12 | async-start | bytes 3145728 | tf_op jit(solution)/shard_map/psum | solution.py:285
  216.0 215.5 %reduce-scatter.24.cloned.1.call-start = ((), (), s32[]{:S(2)}) async-start(), calls=%async_computation.13 | async-start | bytes 1966080 | tf_op jit(solution)/shard_map/reduce_scatter | solution.py:309
  404.1 58.1 %reduce-scatter.26.cloned.1.call-start = ((), (), s32[]{:S(2)}) async-start(), calls=%async_computation.14 | async-start | bytes 1966080 | tf_op jit(solution)/shard_map/reduce_scatter | solution.py:312
  407.9 71.8 %reduce-scatter.40.cloned.1.call-start = ((), (), s32[]{:S(2)}) async-start(), calls=%async_computation.21 | async-start | bytes 884736
  412.7 84.7 %reduce-scatter.36.cloned.1.call-start = ((), (), s32[]{:S(2)}) async-start(), calls=%async_computation.19 | async-start | bytes 884736
  415.6 99.4 %reduce-scatter.38.cloned.1.call-start = ((), (), s32[]{:S(2)}) async-start(), calls=%async_computation.20 | async-start | bytes 884736
  420.9 110.0 %reduce-scatter.34.cloned.1.call-start = ((), (), s32[]{:S(2)}) async-start(), calls=%async_computation.18 | async-start | bytes 589824
  422.6 8.9 %copy-start.27 = (f32[1024,64]{0,1:T(8,128)S(1)}, f32[1024,64]{0,1:T(8,128)}, u32[]{:S(2)}) copy-start(f32[1024,64]{0,1:T(8,128)} %copy-done.26) | copy-start | bytes 786436
  426.6 120.3 %reduce-scatter.30.cloned.1.call-start = ((), (), s32[]{:S(2)}) async-start(), calls=%async_computation.16 | async-start | bytes 589824
  435.8 127.0 %reduce-scatter.28.cloned.1.call-start = ((), (), s32[]{:S(2)}) async-start(), calls=%async_computation.15 | async-start | bytes 589824
  435.8 28.9 %copy-start.41 = (bf16[288,768]{1,0:T(8,128)(2,1)S(1)}, bf16[288,768]{1,0:T(8,128)(2,1)}, u32[]{:S(2)}) copy-start(bf16[288,768]{1,0:T(8,128)(2,1)} %all_gather.43) | copy-start | bytes 1327108
  437.3 141.5 %reduce-scatter.32.cloned.1.call-start = ((), (), s32[]{:S(2)}) async-start(), calls=%async_computation.17 | async-start | bytes 589824
  464.6 157.5 %all-reduce.17.cloned.1.call-start = ((), (), s32[]{:S(2)}) async-start(), calls=%async_computation.23 | async-start | bytes 2506752 | tf_op jit(solution)/shard_map/psum | solution.py:199
  580.5 165.3 %all-reduce.15.cloned.1.call-start = ((), (), s32[]{:S(2)}) async-start(), calls=%async_computation.22 | async-start | bytes 6291456 | tf_op jit(solution)/shard_map/psum | solution.py:275
  586.8 159.1 %copy-start.19 = (f32[1024,768]{1,0:T(8,128)S(1)}, f32[1024,768]{1,0:T(8,128)}, u32[]{:S(2)}) copy-start(f32[1024,768]{1,0:T(8,128)} %get-tuple-element.355) | copy-start | bytes 9437188
  586.8 159.0 %copy-start.51 = (f32[768]{0:T(1024)S(1)}, f32[768]{0:T(1024)}, u32[]{:S(2)}) copy-start(f32[768]{0:T(1024)} %copy-done.50) | copy-start | bytes 9220
  622.1 10.1 %copy-start.45 = (bf16[288,384]{1,0:T(8,128)(2,1)S(1)}, bf16[288,384]{1,0:T(8,128)(2,1)}, u32[]{:S(2)}) copy-start(bf16[288,384]{1,0:T(8,128)(2,1)} %get-tuple-element.338) | copy-start | bytes 663556
  (46 other events, 138.0 us)
Sparse Core Ops, SparseCore 0:
  26.6 21.4 all-gather.6
  50.3 19.6 all-gather.4
  133.2 69.1 all-reduce.10
  216.1 68.1 all-reduce.12
  404.2 27.2 reduce-scatter.23
  434.0 28.1 reduce-scatter.25
  464.5 15.2 reduce-scatter.39
  482.1 15.2 reduce-scatter.35
  499.7 15.2 reduce-scatter.37
  517.8 13.1 reduce-scatter.33
  533.8 13.1 reduce-scatter.29
  549.7 13.1 reduce-scatter.27
  565.6 13.1 reduce-scatter.31
  582.4 39.6 all-reduce.16
  624.4 121.4 all-reduce.14
where the time goes:
time: 805 us; the launch traced here: 797 us
  waiting for transfers between devices  392 us (49%)
  matrix products  134 us (17%)
  local copies, waits for them, and re-layouts  104 us (13%)
  blocking collectives  91.2 us (11%)
  other arithmetic  58.1 us (7%)
  between operations  15.7 us (2%)
    psum x1, waiting for transfers between devices, local(): lax.psum(jnp.dot(hidden, down_w, preferred_element_type=jnp.float32).asty...  113 us
    unnamed x22, waiting for transfers between devices  98.9 us
    psum x1, waiting for transfers between devices, local(): lax.psum((jnp.dot(grad_gate, act_w.T, preferred_element_type=jnp.float32)...  58.2 us
    psum x1, waiting for transfers between devices, local(): lax.psum(jnp.dot(mixed_low, out_w, preferred_element_type=jnp.float32).as...  43.4 us
    unnamed x131, local copies, waits for them, and re-layouts  34.2 us
    psum x1, waiting for transfers between devices, context_total(): lax.psum(query_grad.astype(jnp.bfloat16), 'ctx').astype(jnp.float32)  33.7 us
    psum x1, blocking collectives, local(): lax.psum((gain_first_part, gain_second_grad), ('ctx', 'tp'))  32.3 us
    reduce_scatter x1, waiting for transfers between devices, local(): lax.psum_scatter(value_part.astype(jnp.bfloat16), 'ctx', scatter_dimensio...  24.9 us
  transfers between devices with their start and end apart: 15, of which 14 were waited for; matrix products, arithmetic and copies ran while one was open for 10% of the time, Pallas kernels for 0%

commit v1 on v0

v1 whole, which is shorter than its diff:
```python
import functools
import math

import jax
import jax.numpy as jnp
import numpy as np
from jax import lax
from jax.experimental import pallas as pl
from jax.experimental.pallas import tpu as pltpu
from jax.sharding import PartitionSpec as P

HEAD = 64
EPSILON = 1e-05
ROPE_BASE = 160000.0
MESH = pl.DeviceIdType.MESH
BF = jnp.bfloat16
F32 = jnp.float32
VM = pl.BlockSpec(memory_space=pltpu.VMEM)


def nn(a, b):
    return lax.dot_general(a, b, (((1,), (0,)), ((), ())), preferred_element_type=F32)


def nt(a, b):
    return lax.dot_general(a, b, (((1,), (1,)), ((), ())), preferred_element_type=F32)


def tn(a, b):
    return lax.dot_general(a, b, (((0,), (0,)), ((), ())), preferred_element_type=F32)


def iotas(rows, cols):
    return (
        lax.broadcasted_iota(jnp.int32, (rows, cols), 0),
        lax.broadcasted_iota(jnp.int32, (rows, cols), 1),
    )


def spread(rows, cols, shift):
    i, j = iotas(rows, cols)
    return (j == (i // HEAD) * 128 + i % HEAD + shift).astype(BF)


def gather_cols(rows, cols, shift):
    i, j = iotas(rows, cols)
    return (i == (j // HEAD) * 128 + j % HEAD + shift).astype(BF)


def turn(back):
    i, j = iotas(128, 128)
    if back:
        i, j = j, i
    half = HEAD // 2
    plus = (i == j - half) & (j < HEAD)
    minus = (i == j + half) & (i < HEAD)
    return jnp.where(plus, 1.0, jnp.where(minus, -1.0, 0.0)).astype(BF)


def turned(z, r):
    high = z.astype(BF)
    rest = (z - high.astype(F32)).astype(BF)
    return nn(high, r) + nn(rest, r)


def standardize(x):
    mean_value = jnp.mean(x, axis=-1, keepdims=True)
    centred = x - mean_value
    inverse = lax.rsqrt(jnp.mean(centred * centred, axis=-1, keepdims=True) + EPSILON)
    return centred * inverse, inverse


def norm_back(grad_hat, hat, inverse):
    mean_grad = jnp.mean(grad_hat, axis=-1, keepdims=True)
    mean_cross = jnp.mean(grad_hat * hat, axis=-1, keepdims=True)
    return inverse * (grad_hat - mean_grad - hat * mean_cross)


def greet(peers):
    barrier = pltpu.get_barrier_semaphore()
    for peer in peers:
        pl.semaphore_signal(barrier, inc=1, device_id=peer, device_id_type=MESH)
    pl.semaphore_wait(barrier, len(peers))


def send(src, dst, s_sem, r_sem, peer):
    copy = pltpu.make_async_remote_copy(
        src_ref=src, dst_ref=dst, send_sem=s_sem, recv_sem=r_sem, device_id=peer, device_id_type=MESH
    )
    copy.start()
    return copy


def ring(axis, count):
    me = lax.axis_index(axis)
    return [lax.rem(me + o, count) for o in range(1, count)]


def pairs(dp, ctx):
    d, c = lax.axis_index("dp"), lax.axis_index("ctx")
    return [
        (lax.rem(d + od, dp), lax.rem(c + oc, ctx))
        for od in range(dp)
        for oc in range(ctx)
        if od or oc
    ]


def project_kernel(
    dp, tok, pa, gn, tab, q_out, kv_out, wa, gf, n1, gslot, wq2, gs, gr, ws, wr
):
    rows = tok.shape[0]
    width = tok.shape[1]
    part = pa.shape[0]
    me = lax.axis_index("dp")
    peers = ring("dp", dp)
    greet([{"dp": p} for p in peers])
    copies = []
    for o, p in enumerate(peers):
        copies.append(send(gn, gslot.at[me], gs.at[o], gr.at[o], {"dp": p}))
    weights = []
    for o, p in enumerate(peers):
        weights.append(send(pa, wa.at[me], ws.at[o], wr.at[o], {"dp": p}))
    wa[me] = pa[...]
    gslot[me] = gn[...]
    for c in copies:
        c.wait()
    gains = jnp.zeros((16, width), F32)
    for d in range(dp):
        i, j = iotas(part, width)
        gains = gains + nn(gslot[d], (j == i + d * part).astype(BF))
    gf[...] = gains

    def norm_rows(i, carry):
        at = pl.ds(pl.multiple_of(i * 128, 128), 128)
        hat, _ = standardize(tok[at, :].astype(F32))
        n1[at, :] = (hat * gf[0:1, :]).astype(BF)
        return carry

    lax.fori_loop(0, rows // 128, norm_rows, 0)
    for c in weights:
        c.wait()
    whole = wa[...].reshape(width, wa.shape[2])
    wq2[...] = nn(whole[:, :256], spread(256, 384, 0)).astype(BF)
    r = turn(False)

    def chunk(i, carry):
        at = pl.ds(pl.multiple_of(i * 256, 256), 256)
        x = n1[at, :]
        zq = nn(x, wq2[...])
        zk = nn(x, wa[...].reshape(width, wa.shape[2])[:, 256:])
        cosine, sine = tab[at, 0:128], tab[at, 128:256]
        for h in range(3):
            a = zq[:, h * 128 : (h + 1) * 128]
            q_out[h, at, :] = (0.125 * (a * cosine + turned(a, r) * sine)).astype(BF)
            b = zk[:, h * 128 : (h + 1) * 128]
            kv_out[h, at, :] = (b * cosine + turned(b, r) * sine).astype(BF)
        return carry

    lax.fori_loop(0, rows // 256, chunk, 0)


def attend_kernel(
    dp, tp, q, kv, pb, pc, kvall, mixall, mixf, lse, wb, wo,
    m_s, l_s, acc, vt, ks, kr, bs, br, cs, cr, ts, tr,
):
    rows = q.shape[1]
    d, c, t = lax.axis_index("dp"), lax.axis_index("ctx"), lax.axis_index("tp")
    sib = c + 1 - 2 * lax.rem(c, 2)
    far = lax.rem(c + 2, 4)
    diag = lax.rem(sib + 2, 4)
    dps = ring("dp", dp)
    both = [
        (lax.rem(d + od, dp), lax.rem(t + ot, tp))
        for od in range(dp)
        for ot in range(tp)
        if od or ot
    ]
    greet(
        [{"ctx": sib}, {"ctx": far}] + [{"dp": a, "tp": b} for a, b in both]
    )
    to_far = send(kv, kvall.at[c], ks.at[1], kr.at[1], {"ctx": far})
    to_sib = send(kv, kvall.at[c], ks.at[0], kr.at[0], {"ctx": sib})
    copies = []
    for o, (a, b) in enumerate(both):
        copies.append(send(pc, wo.at[t, d], cs.at[o], cr.at[o], {"dp": a, "tp": b}))
    for o, a in enumerate(dps):
        copies.append(send(pb, wb.at[d], bs.at[o], br.at[o], {"dp": a}))
    wo[t, d] = pc[...]
    wb[d] = pb[...]
    kvall[c] = kv[...]
    m_s[...] = jnp.full(m_s.shape, -1e30, F32)
    l_s[...] = jnp.zeros(l_s.shape, F32)
    acc[...] = jnp.zeros(acc.shape, F32)
    tps = ring("tp", tp)

    def block(step, b):
        def per_head(h, carry):
            vt[...] = kvall[b, h][:, HEAD:].T

            def per_tile(i, inner):
                at = pl.ds(pl.multiple_of(i * 256, 256), 256)
                s = nt(kvall[b, h], q[h, at, :])
                old = m_s[h, 0:1, at]
                new = jnp.maximum(old, jnp.max(s, axis=0, keepdims=True))
                p = jnp.exp(s - new)
                shrink = jnp.exp(old - new)
                m_s[h, 0:1, at] = new
                total = l_s[h, 0:1, at] * shrink + jnp.sum(p, axis=0, keepdims=True)
                l_s[h, 0:1, at] = total
                fresh = acc[h, :, at] * shrink + nn(vt[...], p.astype(BF))
                if step < 3:
                    acc[h, :, at] = fresh
                else:
                    mix = fresh / total
                    mixf[h, :, at] = mix
                    mixall[t, h, :, at] = mix.astype(BF)
                    lse[h, :, at] = jnp.broadcast_to(new + jnp.log(total), (8, 256))
                return inner

            lax.fori_loop(0, rows // 256, per_tile, 0)
            if step == 3:
                for o, p in enumerate(tps):
                    send(
                        mixall.at[t, h], mixall.at[t, h], ts.at[o, h], tr.at[o, h], {"tp": p}
                    )
            return carry

        lax.fori_loop(0, 3, per_head, 0)

    block(0, c)
    to_sib.wait_recv()
    block(1, sib)
    to_far.wait_recv()
    onward = send(kvall.at[far], kvall.at[far], ks.at[2], kr.at[2], {"ctx": sib})
    block(2, far)
    onward.wait_recv()
    block(3, diag)
    to_far.wait_send()
    to_sib.wait_send()
    onward.wait_send()
    for x in copies:
        x.wait()
    for h in range(3):
        for o, p in enumerate(tps):
            pltpu.make_async_remote_copy(
                src_ref=mixall.at[t, h], dst_ref=mixall.at[t, h], send_sem=ts.at[o, h],
                recv_sem=tr.at[o, h], device_id={"tp": p}, device_id_type=MESH,
            ).wait()


def feed_kernel(
    tp, tok, mixall, wo, wb, gf, cot, outp, mid_rows, gm_rows, g128, gall, gain2,
    n2, ggu, hid, gnp, gnr, gml, ss, sr, as_, ar,
):
    rows, width = tok.shape
    unit = rows // tp
    t = lax.axis_index("tp")
    tps = ring("tp", tp)
    greet([{"tp": p} for p in tps])

    def chunk(i, carry):
        c = lax.rem(t + 1 + i, tp)
        at = pl.ds(pl.multiple_of(c * unit, unit), unit)
        middle = tok[at, :].astype(F32)
        for k in range(tp):
            m = mixall[k, :, :, at].reshape(wo.shape[2], unit).T
            middle = middle + nt(m, wo[k])
        mid_rows[...] = middle
        hat, _ = standardize(middle)
        x = (hat * gf[1:2, :]).astype(BF)
        n2[at, :] = x
        w_act, w_up, w_down = wb[0], wb[1], wb[2]
        gate = nn(x, w_act)
        up = nn(x, w_up)
        gh = nn(cot[at, :], w_down)
        cdf = 0.5 * (1.0 + lax.erf(gate * (1.0 / math.sqrt(2.0))))
        density = jnp.exp(-0.5 * gate * gate) * (1.0 / math.sqrt(2.0 * math.pi))
        active = gate * cdf
        hidden = (active * up).astype(BF)
        hid[at, :] = hidden
        gg = (gh * up * (cdf + gate * density)).astype(BF)
        gu = (gh * active).astype(BF)
        ggu[0, at, :] = gg
        ggu[1, at, :] = gu
        gnp[c] = (nt(gg, w_act) + nt(gu, w_up)).astype(BF)
        outp[c] = nt(hidden, w_down).astype(BF)

        @pl.when(i < tp - 1)
        def _():
            send(gnp.at[c], gnr.at[i], ss.at[i], sr.at[i], {"tp": c})

        return carry

    lax.fori_loop(0, tp, chunk, 0)
    gall[0] = tn(n2[...], ggu[0]).astype(BF)
    gall[1] = tn(n2[...], ggu[1]).astype(BF)
    gall[2] = tn(cot[...], hid[...]).astype(BF)
    for o, p in enumerate(tps):
        pltpu.make_async_remote_copy(
            src_ref=gnp.at[p], dst_ref=gnr.at[o], send_sem=ss.at[o], recv_sem=sr.at[o],
            device_id={"tp": p}, device_id_type=MESH,
        ).wait()
    own = gnp[t].astype(F32)
    for o in range(tp - 1):
        own = own + gnr[o].astype(F32)
    hat, inverse = standardize(mid_rows[...])
    gain2[...] = jnp.broadcast_to(jnp.sum(own * hat, axis=0, keepdims=True), gain2.shape)
    at = pl.ds(pl.multiple_of(t * unit, unit), unit)
    gm = cot[at, :].astype(F32) + norm_back(own * gf[1:2, :], hat, inverse)
    gm_rows[...] = gm
    gml[t] = gm.astype(BF)
    copies = [
        send(gml.at[t], gml.at[t], as_.at[o], ar.at[o], {"tp": p}) for o, p in enumerate(tps)
    ]
    wo2 = nn(wo[t], spread(wo.shape[2], 384, HEAD)).astype(BF)
    for x in copies:
        x.wait()
    full = gml[...].reshape(rows, width)
    g = nn(full, wo2).astype(BF)
    for h in range(3):
        g128[h] = g[:, h * 128 : (h + 1) * 128]
    mine = mixall[t].reshape(wo.shape[2], rows)
    og = nn(mine, full).T.astype(BF)
    gall[3] = jnp.concatenate(
        [og, jnp.zeros((width, gall.shape[2] - og.shape[1]), BF)], axis=1
    )


def back_kernel(
    dp, tp, q, g, kvall, mixf, lse, outp, mid_rows, gall, tab, dq, dkv, out_rows, gfin,
    tot, dqt, buf, got, rs, orecv, dsem, drec, wsem, wrec, fsem, frec, osem, orec,
):
    rows = q.shape[1]
    d, c, t = lax.axis_index("dp"), lax.axis_index("ctx"), lax.axis_index("tp")
    sib = c + 1 - 2 * lax.rem(c, 2)
    far = lax.rem(c + 2, 4)
    diag = lax.rem(sib + 2, 4)
    others = pairs(dp, 4)
    tps = ring("tp", tp)
    ctxs = ring("ctx", 4)
    greet([{"dp": a, "ctx": b} for a, b in others] + [{"tp": p} for p in tps])
    outs = [
        send(outp.at[p], orecv.at[o], osem.at[o], orec.at[o], {"tp": p})
        for o, p in enumerate(tps)
    ]
    sums = [
        send(gall.at[b, a], rs.at[o], wsem.at[o], wrec.at[o], {"dp": a, "ctx": b})
        for o, (a, b) in enumerate(others)
    ]
    for h in range(3):
        gt = g[h].astype(F32).T[HEAD:, :]
        tot[h] = jnp.broadcast_to(jnp.sum(gt * mixf[h], axis=0, keepdims=True), (8, rows))
    dqt[...] = jnp.zeros(dqt.shape, F32)

    def block(step, b):
        def per_head(h, carry):
            def per_tile(i, inner):
                at = pl.ds(pl.multiple_of(i * 256, 256), 256)
                k = kvall[b, h, at, :]
                s = nt(k, q[h])
                p = jnp.exp(s - lse[h, 0:1, :])
                gp = nt(k, g[h])
                ds = (p * (gp - tot[h, 0:1, :])).astype(BF)
                buf[step, h, at, :] = (nn(ds, q[h]) + nn(p.astype(BF), g[h])).astype(BF)
                dqt[h] += nn(k[:, :HEAD].T, ds)
                return inner

            lax.fori_loop(0, rows // 256, per_tile, 0)
            return carry

        lax.fori_loop(0, 3, per_head, 0)

    moves = []
    for step, b in enumerate((diag, far, sib)):
        block(step, b)
        moves.append(
            send(buf.at[step], got.at[step], dsem.at[step], drec.at[step], {"ctx": b})
        )
    for x in sums:
        x.wait()
    total = gall[c, d].astype(F32)
    for o in range(len(others)):
        total = total + rs[o].astype(F32)
    gfin[c] = total.astype(BF)
    spreads = [
        send(gfin.at[c], gfin.at[c], fsem.at[o], frec.at[o], {"ctx": p})
        for o, p in enumerate(ctxs)
    ]
    block(3, c)
    r = turn(True)
    for x in outs:
        x.wait()
    own = mid_rows[...] + outp[t].astype(F32)
    for o in range(tp - 1):
        own = own + orecv[o].astype(F32)
    out_rows[...] = own.astype(BF)
    cosine, sine = tab[:, 0:128], tab[:, 128:256]
    for h in range(3):
        z = 0.125 * jnp.concatenate([dqt[h], jnp.zeros((HEAD, rows), F32)], axis=0).T
        dq[h] = (z * cosine + turned(z * sine, r)).astype(BF)
    for x in moves:
        x.wait()
    for h in range(3):
        z = buf[3, h].astype(F32)
        for o in range(3):
            z = z + got[o, h].astype(F32)
        dkv[h] = (z * cosine + turned(z * sine, r)).astype(BF)
    for x in spreads:
        x.wait()


def tail_kernel(
    dp, tp, dq, dkv, n1, tok, gm_rows, wa, gf, gain2, in_rows, gfin, gains,
    wq2, gnp, gnr, gw, rs, gb, gbt, gbc, ss, sr, wsem, wrec, fsem, frec, tsem, trec, csem, crec,
):
    rows, width = n1.shape
    unit = rows // tp
    d, c, t = lax.axis_index("dp"), lax.axis_index("ctx"), lax.axis_index("tp")
    part = width // dp
    others = pairs(dp, 4)
    tps = ring("tp", tp)
    ctxs = ring("ctx", 4)
    greet([{"dp": a, "ctx": b} for a, b in others] + [{"tp": p} for p in tps])
    wq2[...] = nn(wa[:, :256], spread(256, 384, 0)).astype(BF)

    def chunk(i, carry):
        r = lax.rem(t + 1 + i, tp)
        at = pl.ds(pl.multiple_of(r * unit, unit), unit)
        total = jnp.zeros((unit, width), F32)
        for h in range(3):
            cols = slice(h * 128, (h + 1) * 128)
            total = total + nt(dq[h, at, :], wq2[:, cols])
            total = total + nt(dkv[h, at, :], wa[:, 256 + h * 128 : 384 + h * 128])
        gnp[r] = total.astype(BF)

        @pl.when(i < tp - 1)
        def _():
            send(gnp.at[r], gnr.at[i], ss.at[i], sr.at[i], {"tp": r})

        return carry

    lax.fori_loop(0, tp, chunk, 0)
    n1t = n1[...].T
    gq = jnp.concatenate([nn(n1t, dq[h]).astype(BF) for h in range(3)], axis=1)
    gkv = jnp.concatenate([nn(n1t, dkv[h]).astype(BF) for h in range(3)], axis=1)
    low, high = gather_cols(384, 192, 0), gather_cols(384, 192, HEAD)
    gw[0] = nn(gq, low).astype(BF).reshape(dp, part, 192)
    gw[1] = nn(gkv, low).astype(BF).reshape(dp, part, 192)
    gw[2] = nn(gkv, high).astype(BF).reshape(dp, part, 192)

    def owner_copy(o, a, b):
        return pltpu.make_async_remote_copy(
            src_ref=gw.at[b, a], dst_ref=rs.at[o], send_sem=wsem.at[o], recv_sem=wrec.at[o],
            device_id={"dp": a, "ctx": b}, device_id_type=MESH,
        )

    for o, (a, b) in enumerate(others):
        @pl.when(b < 3)
        def _(o=o, a=a, b=b):
            owner_copy(o, a, b).start()

    for o, p in enumerate(tps):
        pltpu.make_async_remote_copy(
            src_ref=gnp.at[p], dst_ref=gnr.at[o], send_sem=ss.at[o], recv_sem=sr.at[o],
            device_id={"tp": p}, device_id_type=MESH,
        ).wait()
    own = gnp[t].astype(F32)
    for o in range(tp - 1):
        own = own + gnr[o].astype(F32)
    at = pl.ds(pl.multiple_of(t * unit, unit), unit)
    hat, inverse = standardize(tok[at, :].astype(F32))
    first = jnp.sum(own * hat, axis=0, keepdims=True)
    gb[...] = jnp.concatenate([first, gain2[0:1, :], jnp.zeros((6, width), F32)], axis=0)
    small = [send(gb, gbt.at[o], tsem.at[o], trec.at[o], {"tp": p}) for o, p in enumerate(tps)]
    in_rows[...] = (gm_rows[...] + norm_back(own * gf[0:1, :], hat, inverse)).astype(BF)
    for x in small:
        x.wait()
    total = gb[...]
    for o in range(tp - 1):
        total = total + gbt[o]
    gb[...] = total
    wide = [
        send(gb, gbc.at[o], csem.at[o], crec.at[o], {"dp": a, "ctx": b})
        for o, (a, b) in enumerate(others)
    ]

    @pl.when(c < 3)
    def _():
        for o, (a, b) in enumerate(others):
            owner_copy(o, a, 0).wait_recv()
        w = gw[c, d].astype(F32)
        for o in range(len(others)):
            w = w + rs[o].astype(F32)
        gfin[c] = w.astype(BF)
        for o, p in enumerate(ctxs):
            send(gfin.at[c], gfin.at[c], fsem.at[o], frec.at[o], {"ctx": p})

    for x in wide:
        x.wait()
    total = gb[...]
    for o in range(len(others)):
        total = total + gbc[o]
    gains[...] = total
    for o, (a, b) in enumerate(others):
        @pl.when(b < 3)
        def _(o=o, a=a, b=b):
            owner_copy(o, a, b).wait_send()

    def final_copy(o, p, slot):
        return pltpu.make_async_remote_copy(
            src_ref=gfin.at[slot], dst_ref=gfin.at[slot], send_sem=fsem.at[o],
            recv_sem=frec.at[o], device_id={"ctx": p}, device_id_type=MESH,
        )

    for o, p in enumerate(ctxs):
        origin = lax.rem(c + 4 - (o + 1), 4)

        @pl.when(origin < 3)
        def _(o=o, p=p, origin=origin):
            final_copy(o, p, origin).wait_recv()

    @pl.when(c < 3)
    def _():
        for o, p in enumerate(ctxs):
            final_copy(o, p, c).wait_send()


def call(kernel, number, outs, scratch, flops, *args):
    return pl.pallas_call(
        kernel,
        out_shape=[jax.ShapeDtypeStruct(s, t) for s, t in outs],
        in_specs=[VM] * len(args),
        out_specs=[VM] * len(outs),
        scratch_shapes=[
            pltpu.SemaphoreType.DMA(s) if t is None else pltpu.VMEM(s, t) for s, t in scratch
        ],
        compiler_params=pltpu.CompilerParams(
            collective_id=number, has_side_effects=True, vmem_limit_bytes=56 * 2**20
        ),
        cost_estimate=pl.CostEstimate(flops=flops, bytes_accessed=10**7, transcendentals=0),
    )(*args)


def local(
    dp, ctx, tp, tokens, w_query, w_key, w_value, w_out, w_act, w_up, w_down, gain_one, gain_two,
    cotangent,
):
    T, D = tokens.shape
    part = w_query.shape[0]
    feat = w_query.shape[1]
    hidden = w_act.shape[1]
    unit = T // tp
    pad = jnp.zeros((part, HEAD), BF)
    mixed = [w_query, pad]
    for h in range(3):
        at = slice(h * HEAD, (h + 1) * HEAD)
        mixed += [w_key[:, at], w_value[:, at]]
    pa = jnp.concatenate(mixed, axis=1)
    gn = jnp.concatenate([gain_one[None], gain_two[None], jnp.zeros((14, part), BF)], axis=0)
    pb = jnp.stack([w_act, w_up, w_down.T])
    pc = w_out.T
    position = np.arange(ctx * T, dtype=np.float32)
    frequency = (ROPE_BASE ** (-np.arange(0, HEAD, 2) / HEAD)).astype(np.float32)
    angle = (position[:, None] * frequency[None, :]).astype(np.float64)
    cosine, sine = np.cos(angle), np.sin(angle)
    table = np.concatenate(
        [cosine, cosine, np.ones((ctx * T, HEAD)), sine, sine, np.zeros((ctx * T, HEAD))], axis=1
    ).astype(np.float32)
    tab = lax.dynamic_slice_in_dim(jnp.asarray(table), lax.axis_index("ctx") * T, T, 0)
    n_d, n_t, n_dt, n_dc = dp - 1, tp - 1, dp * tp - 1, dp * ctx - 1
    q, kv, wa, gf, n1 = call(
        functools.partial(project_kernel, dp), 1,
        [((3, T, 128), BF), ((3, T, 128), BF), ((dp, part, 640), BF), ((16, D), F32), ((T, D), BF)],
        [((dp, 16, part), BF), ((D, 384), BF)] + [((n_d,), None)] * 4, 10**9,
        tokens, pa, gn, tab,
    )
    kvall, mixall, mixf, lse, wb, wo = call(
        functools.partial(attend_kernel, dp, tp), 2,
        [
            ((ctx, 3, T, 128), BF), ((tp, 3, HEAD, T), BF), ((3, HEAD, T), F32), ((3, 8, T), F32),
            ((dp, 3, part, hidden), BF), ((tp, dp, part, feat), BF),
        ],
        [((3, 8, T), F32), ((3, 8, T), F32), ((3, HEAD, T), F32), ((HEAD, T), BF)]
        + [((3,), None)] * 2 + [((n_d,), None)] * 2 + [((n_dt,), None)] * 2
        + [((n_t, 3), None)] * 2, 10**10,
        q, kv, pb, pc,
    )
    wb = jnp.transpose(wb, (1, 0, 2, 3)).reshape(3, D, hidden)
    wo = wo.reshape(tp, D, feat)
    outp, mid_rows, gm_rows, g128, gall, gain2 = call(
        functools.partial(feed_kernel, tp), 3,
        [
            ((tp, unit, D), BF), ((unit, D), F32), ((unit, D), F32), ((3, T, 128), BF),
            ((4, D, hidden), BF), ((8, D), F32),
        ],
        [
            ((T, D), BF), ((2, T, hidden), BF), ((T, hidden), BF), ((tp, unit, D), BF),
            ((n_t, unit, D), BF), ((tp, unit, D), BF),
        ] + [((n_t,), None)] * 4, 10**10,
        tokens, mixall, wo, wb, gf, cotangent,
    )
    dq, dkv, out_rows, gfin = call(
        functools.partial(back_kernel, dp, tp), 4,
        [((3, T, 128), BF), ((3, T, 128), BF), ((unit, D), BF), ((4, part, hidden), BF)],
        [
            ((3, 8, T), F32), ((3, HEAD, T), F32), ((4, 3, T, 128), BF), ((3, 3, T, 128), BF),
            ((n_dc, part, hidden), BF), ((n_t, unit, D), BF),
        ] + [((3,), None)] * 2 + [((n_dc,), None)] * 2 + [((3,), None)] * 2 + [((n_t,), None)] * 2,
        10**10,
        q, g128, kvall, mixf, lse, outp, mid_rows, gall.reshape(4, dp, part, hidden), tab,
    )
    in_rows, gqkv, gains = call(
        functools.partial(tail_kernel, dp, tp), 5,
        [((unit, D), BF), ((3, part, feat), BF), ((8, D), F32)],
        [
            ((D, 384), BF), ((tp, unit, D), BF), ((n_t, unit, D), BF), ((3, dp, part, feat), BF),
            ((n_dc, part, feat), BF), ((8, D), F32), ((n_t, 8, D), F32), ((n_dc, 8, D), F32),
        ] + [((n_t,), None)] * 2 + [((n_dc,), None)] * 2 + [((3,), None)] * 2
        + [((n_t,), None)] * 2 + [((n_dc,), None)] * 2, 10**10,
        dq, dkv, n1, tokens, gm_rows, wa.reshape(D, 640), gf, gain2,
    )
    own = lax.dynamic_slice_in_dim(gains[:2], lax.axis_index("dp") * part, part, 1)
    return (
        out_rows,
        in_rows,
        gqkv[0].astype(F32),
        gqkv[1].astype(F32),
        gqkv[2].astype(F32),
        gfin[3][:, :feat].T.astype(F32),
        gfin[0].astype(F32),
        gfin[1].astype(F32),
        gfin[2].T.astype(F32),
        own[0],
        own[1],
    )


def solution(mesh):
    in_specs = (
        P(("dp", "ctx"), None),
        P("dp", "tp"),
        P("dp", "tp"),
        P("dp", "tp"),
        P("tp", "dp"),
        P("dp", "tp"),
        P("dp", "tp"),
        P("tp", "dp"),
        P("dp"),
        P("dp"),
        P(("dp", "ctx"), None),
    )
    out_specs = (
        P(("dp", "ctx", "tp"), None),
        P(("dp", "ctx", "tp"), None),
        P("dp", "tp"),
        P("dp", "tp"),
        P("dp", "tp"),
        P("tp", "dp"),
        P("dp", "tp"),
        P("dp", "tp"),
        P("tp", "dp"),
        P("dp"),
        P("dp"),
    )
    body = functools.partial(local, mesh.shape["dp"], mesh.shape["ctx"], mesh.shape["tp"])
    return jax.shard_map(body, mesh=mesh, in_specs=in_specs, out_specs=out_specs, check_vma=False)
```

time: 805 us -> 346 us (0.43)
  waiting for transfers between devices: 392 us -> 0 us
  Pallas kernels: 0 us -> 322 us
  matrix products: 134 us -> 0 us
  blocking collectives: 91.2 us -> 0 us
  local copies, waits for them, and re-layouts: 104 us -> 19.8 us
  other arithmetic: 58.1 us -> 3.29 us
  between operations: 15.7 us -> 0.86 us
    pallas_call x0 -> x5, Pallas kernels: none -> 322 us  [call(): pl.pallas_call(kernel, out_shape=[jax.ShapeDtypeStruct(s, t) for s, t in...]
    psum x4 -> x0, waiting for transfers between devices: 248 us -> none  [the longest x1 113 us: local(): lax.psum(jnp.dot(hidden, down_w, preferred_element_type=jnp.float32).asty...]
    dot_general x65 -> x0, matrix products: 134 us -> none  [the longest x8 23.3 us: per_key(): jnp.einsum('qhd,khd->hqk', grad_block, value_block, preferred_element_typ...]
    unnamed x22 -> x0, waiting for transfers between devices: 98.9 us -> none
    all_gather x9 -> x0, blocking collectives: 53.9 us -> none  [the longest x1 7.2 us: local(): lax.all_gather(w_act, 'dp', axis=0, tiled=True)]
    psum x1 -> x0, blocking collectives: 32.3 us -> none  [local(): lax.psum((gain_first_part, gain_second_grad), ('ctx', 'tp'))]
    reduce_scatter x2 -> x0, waiting for transfers between devices: 29.7 us -> none  [the longest x1 24.9 us: local(): lax.psum_scatter(value_part.astype(jnp.bfloat16), 'ctx', scatter_dimensio...]
    dynamic_update_slice x8 -> x0, local copies, waits for them, and re-layouts: 24.8 us -> none  [the longest x4 16.9 us: attend_back(): lax.scan(per_query, (zero_blocks, zero_blocks), (query_blocks, grad_block...]
  transfers between devices with their start and end apart: 15 -> 0, of which waited for: 14 -> 0; matrix products, arithmetic and copies ran while one was open for 10% -> 0% of each run, Pallas kernels for 0% -> 0%
where the time goes in v1:
time: 346 us; the launch traced here: 345 us
  Pallas kernels  322 us (93%)
  local copies, waits for them, and re-layouts  19.8 us (6%)
    pallas_call x5, Pallas kernels, call(): pl.pallas_call(kernel, out_shape=[jax.ShapeDtypeStruct(s, t) for s, t in...  322 us
    unnamed x40, local copies, waits for them, and re-layouts  10.3 us

profile of v1, /device:TPU:0, one launch (start us, length us, event | category | flops | bytes accessed | tf_op | source)
XLA Modules:
  0.0 345.5 jit_solution(7423728243454889053)
XLA Ops:
  0.7 0.9 fusion.1
  1.6 0.1 copy.42
  1.7 0.9 fusion
  2.5 0.1 copy.43
  3.2 0.1 copy.29
  3.4 1.1 concatenate.6.pa
  4.5 2.3 constant_dynamic-slice_fusion.tab
  6.9 0.7 maximum_maximum_fusion.gn
  7.6 22.1 %shard_map.203 = (bf16[3,1024,128]{2,1,0:T(8,128)(2,1)}, bf16[3,1024,128]{2,1,0:T(8,128)(2,1)}, bf16[2,384,640]{2,1,0:T(8,128)(2,1)}, f32[16,768]{1,0:T(8,128)}, bf16[1024,768]{1,0:T(8,128)(2,1)}) custom-call(bf16[1024,768]{1,0:T(8,128)(2,1)} %tok.5, bf16[384,640]{1,0:T(8,128)(2,1)} %concatenate.6.pa, bf16[16,384]{1,0:T(8,128)(2,1)} %maximum_maximum_fusion.gn, ...), custom_call_target="tpu_custom_call" | custom-call | flops 1000000000 | bytes 10000000 | tf_op jit(solution)/shard_map/pallas_call | solution.py:530
  29.6 0.2 copy.30
  29.9 0.2 copy.31
  30.1 0.2 copy.32
  30.3 1.1 pad_maximum_fusion.pb
  31.5 0.8 copy.33
  32.3 75.6 %shard_map.204 = (bf16[4,3,1024,128]{3,2,1,0:T(8,128)(2,1)}, bf16[4,3,64,1024]{3,2,1,0:T(8,128)(2,1)}, f32[3,64,1024]{2,1,0:T(8,128)}, f32[3,8,1024]{2,1,0:T(8,1...) custom-call(bf16[3,1024,128]{2,1,0:T(8,128)(2,1)} %get-tuple-element.35.q, ...), custom_call_target="tpu_custom_call" | custom-call | flops 10000000000 | bytes 10000000 | tf_op jit(solution)/shard_map/pallas_call | solution.py:530
  107.9 2.9 copy.34
  110.7 79.7 %shard_map.205 = (bf16[4,256,768]{2,1,0:T(8,128)(2,1)}, f32[256,768]{1,0:T(8,128)}, f32[256,768]{1,0:T(8,128)}, bf16[3,1024,128]{2,1,0:T(8,128)(2,1)}, bf16[4,768,288]{2,1,0:T(8,128)(2,1)}, /*index=5*/f32[8,768]{1,0:T(8,128)}) custom-call(bf16[1024,768]{1,0:T(8,128)(2,1)} %tok.5, bf16[4,3,64,1024]{3,2,1,0:T(8,128)(2,1)} %get-tuple-element.37.mixall, ...), custom_call_target="tpu_custom_call" | custom-call | flops 10000000000 | bytes 10000000 | tf_op jit(solution)/shard_map/pallas_call | solution.py:530
  190.5 85.5 %shard_map.206 = (bf16[3,1024,128]{2,1,0:T(8,128)(2,1)}, bf16[3,1024,128]{2,1,0:T(8,128)(2,1)}, bf16[256,768]{1,0:T(8,128)(2,1)}, bf16[4,384,288]{2,1,0:T(8,128)(2,1)}) custom-call(bf16[3,1024,128]{2,1,0:T(8,128)(2,1)} %get-tuple-element.35.q, bf16[3,1024,128]{2,1,0:T(8,128)(2,1)} %get-tuple-element.41.g, bf16[4,3,1024,128]{3,2,1,0:T(8,128)(2,1)} %get-tuple-element.42.kvall, ...), custom_call_target="tpu_custom_call" | custom-call | flops 10000000000 | bytes 10000000 | tf_op jit(solution)/shard_map/pallas_call | solution.py:530
  275.9 58.7 %shard_map.207 = (bf16[256,768]{1,0:T(8,128)(2,1)}, bf16[3,384,192]{2,1,0:T(8,128)(2,1)}, f32[8,768]{1,0:T(8,128)}) custom-call(bf16[3,1024,128]{2,1,0:T(8,128)(2,1)} %get-tuple-element.49.dq, bf16[3,1024,128]{2,1,0:T(8,128)(2,1)} %get-tuple-element.50.dkv, bf16[1024,768]{1,0:T(8,128)(2,1)} %get-tuple-element.51.n1, bf16[1024,768]{1,0:T(8,128)(2,1)} %tok.5, ...), custom_call_target="tpu_custom_call" | custom-call | flops 10000000000 | bytes 10000000 | tf_op jit(solution)/shard_map/pallas_call | solution.py:530
  334.7 1.3 bitcast_convert_fusion.2
  336.0 0.9 copy.35
  336.9 0.9 copy.36
  337.7 0.9 copy.37
  338.6 0.1 convert_bitcast_fusion
  338.8 0.9 copy.38
  339.6 1.0 copy.39
  340.6 1.0 copy.40
  341.6 1.0 copy.41
  342.6 0.7 slice.65
  343.3 0.7 dynamic-slice_reduce_fusion
  344.0 0.7 copy.50
  344.7 0.7 copy.51
  (30 shorter events, 0.7 us)
Async XLA Ops:
  0.6 2.5 copy-start.6
  3.4 3.4 copy-start.8
  3.4 3.4 copy-start.9
  7.5 22.1 %copy-start.3 = (bf16[384,288]{0,1:T(8,128)(2,1)S(1)}, bf16[384,288]{0,1:T(8,128)(2,1)}, u32[]{:S(2)}) copy-start(bf16[384,288]{0,1:T(8,128)(2,1)} %param.17) | copy-start | bytes 663556
  7.5 22.3 %copy-start.4 = (bf16[384,288]{0,1:T(8,128)(2,1)S(1)}, bf16[384,288]{0,1:T(8,128)(2,1)}, u32[]{:S(2)}) copy-start(bf16[384,288]{0,1:T(8,128)(2,1)} %param.18) | copy-start | bytes 663556
  7.6 22.5 %copy-start.5 = (bf16[288,384]{1,0:T(8,128)(2,1)S(1)}, bf16[288,384]{1,0:T(8,128)(2,1)}, u32[]{:S(2)}) copy-start(bf16[288,384]{1,0:T(8,128)(2,1)} %param.19) | copy-start | bytes 663556
  29.6 1.8 copy-start.7
  334.7 3.9 %copy-start = (bf16[4,384,288]{2,1,0:T(8,128)(2,1)S(1)}, bf16[4,384,288]{2,1,0:T(8,128)(2,1)}, u32[]{:S(2)}) copy-start(bf16[4,384,288]{2,1,0:T(8,128)(2,1)} %get-tuple-element.57) | copy-start | bytes 2654212
  339.6 4.3 %copy-start.1 = (bf16[256,768]{1,0:T(8,128)(2,1)S(1)}, bf16[256,768]{1,0:T(8,128)(2,1)}, u32[]{:S(2)}) copy-start(bf16[256,768]{1,0:T(8,128)(2,1)} %get-tuple-element.96) | copy-start | bytes 1179652
  340.6 4.1 %copy-start.2 = (bf16[256,768]{1,0:T(8,128)(2,1)S(1)}, bf16[256,768]{1,0:T(8,128)(2,1)}, u32[]{:S(2)}) copy-start(bf16[256,768]{1,0:T(8,128)(2,1)} %get-tuple-element.97) | copy-start | bytes 1179652

commit v2 on v1

--- a/solution.py
+++ b/solution.py
@@ -185,17 +185,28 @@
     for o, (a, b) in enumerate(both):
         copies.append(send(pc, wo.at[t, d], cs.at[o], cr.at[o], {"dp": a, "tp": b}))
     for o, a in enumerate(dps):
-        copies.append(send(pb, wb.at[d], bs.at[o], br.at[o], {"dp": a}))
+        copies.append(send(pb, wb.at[:, d], bs.at[o], br.at[o], {"dp": a}))
     wo[t, d] = pc[...]
-    wb[d] = pb[...]
+    for m in range(3):
+        wb[m, d] = pb[m]
     kvall[c] = kv[...]
     m_s[...] = jnp.full(m_s.shape, -1e30, F32)
     l_s[...] = jnp.zeros(l_s.shape, F32)
     acc[...] = jnp.zeros(acc.shape, F32)
     tps = ring("tp", tp)
 
-    def block(step, b):
+    def block(*steps):
         def per_head(h, carry):
+            for step, b in steps:
+                one(step, b, h)
+            if steps[-1][0] == 3:
+                for o, p in enumerate(tps):
+                    send(
+                        mixall.at[t, h], mixall.at[t, h], ts.at[o, h], tr.at[o, h], {"tp": p}
+                    )
+            return carry
+
+        def one(step, b, h):
             vt[...] = kvall[b, h][:, HEAD:].T
 
             def per_tile(i, inner):
@@ -219,23 +230,16 @@
                 return inner
 
             lax.fori_loop(0, rows // 256, per_tile, 0)
-            if step == 3:
-                for o, p in enumerate(tps):
-                    send(
-                        mixall.at[t, h], mixall.at[t, h], ts.at[o, h], tr.at[o, h], {"tp": p}
-                    )
-            return carry
 
         lax.fori_loop(0, 3, per_head, 0)
 
-    block(0, c)
+    block((0, c))
     to_sib.wait_recv()
-    block(1, sib)
     to_far.wait_recv()
     onward = send(kvall.at[far], kvall.at[far], ks.at[2], kr.at[2], {"ctx": sib})
-    block(2, far)
+    block((1, sib))
     onward.wait_recv()
-    block(3, diag)
+    block((2, far), (3, diag))
     to_far.wait_send()
     to_sib.wait_send()
     onward.wait_send()
@@ -250,8 +254,8 @@
 
 
 def feed_kernel(
-    tp, tok, mixall, wo, wb, gf, cot, outp, mid_rows, gm_rows, g128, gall, gain2,
-    n2, ggu, hid, gnp, gnr, gml, ss, sr, as_, ar,
+    tp, tok, mixall, wo, wb, gf, cot, outp, mid_rows, gm_rows, g128, gall, gain2, gml,
+    n2, ggu, hid, gnp, gnr, gsend, wo2, ss, sr, as_, ar,
 ):
     rows, width = tok.shape
     unit = rows // tp
@@ -309,27 +313,27 @@
     at = pl.ds(pl.multiple_of(t * unit, unit), unit)
     gm = cot[at, :].astype(F32) + norm_back(own * gf[1:2, :], hat, inverse)
     gm_rows[...] = gm
-    gml[t] = gm.astype(BF)
-    copies = [
-        send(gml.at[t], gml.at[t], as_.at[o], ar.at[o], {"tp": p}) for o, p in enumerate(tps)
-    ]
-    wo2 = nn(wo[t], spread(wo.shape[2], 384, HEAD)).astype(BF)
+    gml[...] = gm.astype(BF)
+    copies = []
+    for o in list(range(1, tp)) + [0]:
+        p = lax.rem(t + o, tp)
+        gsend[p] = nn(gml[...], wo[p]).astype(BF)
+        if o:
+            copies.append(
+                send(gsend.at[p], wo2.at[t], as_.at[o - 1], ar.at[o - 1], {"tp": p})
+            )
+    wo2[t] = gsend[t]
+    spacing = spread(wo.shape[2], 384, HEAD)
     for x in copies:
         x.wait()
-    full = gml[...].reshape(rows, width)
-    g = nn(full, wo2).astype(BF)
+    g = nn(wo2[...].reshape(rows, wo.shape[2]), spacing).astype(BF)
     for h in range(3):
         g128[h] = g[:, h * 128 : (h + 1) * 128]
-    mine = mixall[t].reshape(wo.shape[2], rows)
-    og = nn(mine, full).T.astype(BF)
-    gall[3] = jnp.concatenate(
-        [og, jnp.zeros((width, gall.shape[2] - og.shape[1]), BF)], axis=1
-    )
 
 
 def back_kernel(
-    dp, tp, q, g, kvall, mixf, lse, outp, mid_rows, gall, tab, dq, dkv, out_rows, gfin,
-    tot, dqt, buf, got, rs, orecv, dsem, drec, wsem, wrec, fsem, frec, osem, orec,
+    dp, tp, q, g, kvall, mixf, lse, outp, mid_rows, gall, tab, gml, dq, dkv, out_rows, gfin, gmlall,
+    tot, dqt, buf, got, rs, orecv, dsem, drec, wsem, wrec, fsem, frec, osem, orec, asem, arec,
 ):
     rows = q.shape[1]
     d, c, t = lax.axis_index("dp"), lax.axis_index("ctx"), lax.axis_index("tp")
@@ -344,10 +348,22 @@
         send(outp.at[p], orecv.at[o], osem.at[o], orec.at[o], {"tp": p})
         for o, p in enumerate(tps)
     ]
-    sums = [
-        send(gall.at[b, a], rs.at[o], wsem.at[o], wrec.at[o], {"dp": a, "ctx": b})
-        for o, (a, b) in enumerate(others)
+    outs += [
+        send(gml, gmlall.at[t], asem.at[o], arec.at[o], {"tp": p}) for o, p in enumerate(tps)
     ]
+    gmlall[t] = gml[...]
+
+    def owner_copy(o, a, b):
+        return pltpu.make_async_remote_copy(
+            src_ref=gall.at[b, a], dst_ref=rs.at[o], send_sem=wsem.at[o], recv_sem=wrec.at[o],
+            device_id={"dp": a, "ctx": b}, device_id_type=MESH,
+        )
+
+    for o, (a, b) in enumerate(others):
+        @pl.when(b < 3)
+        def _(o=o, a=a, b=b):
+            owner_copy(o, a, b).start()
+
     for h in range(3):
         gt = g[h].astype(F32).T[HEAD:, :]
         tot[h] = jnp.broadcast_to(jnp.sum(gt * mixf[h], axis=0, keepdims=True), (8, rows))
@@ -377,16 +393,17 @@
         moves.append(
             send(buf.at[step], got.at[step], dsem.at[step], drec.at[step], {"ctx": b})
         )
-    for x in sums:
-        x.wait()
-    total = gall[c, d].astype(F32)
-    for o in range(len(others)):
-        total = total + rs[o].astype(F32)
-    gfin[c] = total.astype(BF)
-    spreads = [
-        send(gfin.at[c], gfin.at[c], fsem.at[o], frec.at[o], {"ctx": p})
-        for o, p in enumerate(ctxs)
-    ]
+    @pl.when(c < 3)
+    def _():
+        for o, (a, b) in enumerate(others):
+            owner_copy(o, a, 0).wait_recv()
+        total = gall[c, d].astype(F32)
+        for o in range(len(others)):
+            total = total + rs[o].astype(F32)
+        gfin[c] = total.astype(BF)
+        for o, p in enumerate(ctxs):
+            send(gfin.at[c], gfin.at[c], fsem.at[o], frec.at[o], {"ctx": p})
+
     block(3, c)
     r = turn(True)
     for x in outs:
@@ -406,12 +423,32 @@
         for o in range(3):
             z = z + got[o, h].astype(F32)
         dkv[h] = (z * cosine + turned(z * sine, r)).astype(BF)
-    for x in spreads:
-        x.wait()
+    for o, (a, b) in enumerate(others):
+        @pl.when(b < 3)
+        def _(o=o, a=a, b=b):
+            owner_copy(o, a, b).wait_send()
+
+    def final_copy(o, p, slot):
+        return pltpu.make_async_remote_copy(
+            src_ref=gfin.at[slot], dst_ref=gfin.at[slot], send_sem=fsem.at[o],
+            recv_sem=frec.at[o], device_id={"ctx": p}, device_id_type=MESH,
+        )
+
+    for o, p in enumerate(ctxs):
+        origin = lax.rem(c + 4 - (o + 1), 4)
+
+        @pl.when(origin < 3)
+        def _(o=o, p=p, origin=origin):
+            final_copy(o, p, origin).wait_recv()
+
+    @pl.when(c < 3)
+    def _():
+        for o, p in enumerate(ctxs):
+            final_copy(o, p, c).wait_send()
 
 
 def tail_kernel(
-    dp, tp, dq, dkv, n1, tok, gm_rows, wa, gf, gain2, in_rows, gfin, gains,
+    dp, tp, dq, dkv, n1, tok, gm_rows, wa, gf, gain2, mixall, gml, in_rows, gfin, gains,
     wq2, gnp, gnr, gw, rs, gb, gbt, gbc, ss, sr, wsem, wrec, fsem, frec, tsem, trec, csem, crec,
 ):
     rows, width = n1.shape
@@ -448,18 +485,23 @@
     gw[0] = nn(gq, low).astype(BF).reshape(dp, part, 192)
     gw[1] = nn(gkv, low).astype(BF).reshape(dp, part, 192)
     gw[2] = nn(gkv, high).astype(BF).reshape(dp, part, 192)
-
-    def owner_copy(o, a, b):
-        return pltpu.make_async_remote_copy(
-            src_ref=gw.at[b, a], dst_ref=rs.at[o], send_sem=wsem.at[o], recv_sem=wrec.at[o],
-            device_id={"dp": a, "ctx": b}, device_id_type=MESH,
-        )
-
-    for o, (a, b) in enumerate(others):
-        @pl.when(b < 3)
-        def _(o=o, a=a, b=b):
-            owner_copy(o, a, b).start()
-
+    mine = mixall[t].reshape(192, rows)
+    gw[3] = nn(mine, gml[...].reshape(rows, width)).T.astype(BF).reshape(dp, part, 192)
+
+    sums = [
+        send(gw.at[b, a], rs.at[o], wsem.at[o], wrec.at[o], {"dp": a, "ctx": b})
+        for o, (a, b) in enumerate(others)
+    ]
+    for x in sums:
+        x.wait()
+    w = gw[c, d].astype(F32)
+    for o in range(len(others)):
+        w = w + rs[o].astype(F32)
+    gfin[c] = w.astype(BF)
+    spreads = [
+        send(gfin.at[c], gfin.at[c], fsem.at[o], frec.at[o], {"ctx": p})
+        for o, p in enumerate(ctxs)
+    ]
     for o, p in enumerate(tps):
         pltpu.make_async_remote_copy(
             src_ref=gnp.at[p], dst_ref=gnr.at[o], send_sem=ss.at[o], recv_sem=sr.at[o],
@@ -484,46 +526,14 @@
         send(gb, gbc.at[o], csem.at[o], crec.at[o], {"dp": a, "ctx": b})
         for o, (a, b) in enumerate(others)
     ]
-
-    @pl.when(c < 3)
-    def _():
-        for o, (a, b) in enumerate(others):
-            owner_copy(o, a, 0).wait_recv()
-        w = gw[c, d].astype(F32)
-        for o in range(len(others)):
-            w = w + rs[o].astype(F32)
-        gfin[c] = w.astype(BF)
-        for o, p in enumerate(ctxs):
-            send(gfin.at[c], gfin.at[c], fsem.at[o], frec.at[o], {"ctx": p})
-
     for x in wide:
         x.wait()
     total = gb[...]
     for o in range(len(others)):
         total = total + gbc[o]
     gains[...] = total
-    for o, (a, b) in enumerate(others):
-        @pl.when(b < 3)
-        def _(o=o, a=a, b=b):
-            owner_copy(o, a, b).wait_send()
-
-    def final_copy(o, p, slot):
-        return pltpu.make_async_remote_copy(
-            src_ref=gfin.at[slot], dst_ref=gfin.at[slot], send_sem=fsem.at[o],
-            recv_sem=frec.at[o], device_id={"ctx": p}, device_id_type=MESH,
-        )
-
-    for o, p in enumerate(ctxs):
-        origin = lax.rem(c + 4 - (o + 1), 4)
-
-        @pl.when(origin < 3)
-        def _(o=o, p=p, origin=origin):
-            final_copy(o, p, origin).wait_recv()
-
-    @pl.when(c < 3)
-    def _():
-        for o, p in enumerate(ctxs):
-            final_copy(o, p, c).wait_send()
+    for x in spreads:
+        x.wait()
 
 
 def call(kernel, number, outs, scratch, flops, *args):
@@ -579,46 +589,46 @@
         functools.partial(attend_kernel, dp, tp), 2,
         [
             ((ctx, 3, T, 128), BF), ((tp, 3, HEAD, T), BF), ((3, HEAD, T), F32), ((3, 8, T), F32),
-            ((dp, 3, part, hidden), BF), ((tp, dp, part, feat), BF),
+            ((3, dp, part, hidden), BF), ((tp, dp, part, feat), BF),
         ],
         [((3, 8, T), F32), ((3, 8, T), F32), ((3, HEAD, T), F32), ((HEAD, T), BF)]
         + [((3,), None)] * 2 + [((n_d,), None)] * 2 + [((n_dt,), None)] * 2
         + [((n_t, 3), None)] * 2, 10**10,
         q, kv, pb, pc,
     )
-    wb = jnp.transpose(wb, (1, 0, 2, 3)).reshape(3, D, hidden)
+    wb = wb.reshape(3, D, hidden)
     wo = wo.reshape(tp, D, feat)
-    outp, mid_rows, gm_rows, g128, gall, gain2 = call(
+    outp, mid_rows, gm_rows, g128, gall, gain2, gml = call(
         functools.partial(feed_kernel, tp), 3,
         [
             ((tp, unit, D), BF), ((unit, D), F32), ((unit, D), F32), ((3, T, 128), BF),
-            ((4, D, hidden), BF), ((8, D), F32),
+            ((3, D, hidden), BF), ((8, D), F32), ((unit, D), BF),
         ],
         [
             ((T, D), BF), ((2, T, hidden), BF), ((T, hidden), BF), ((tp, unit, D), BF),
-            ((n_t, unit, D), BF), ((tp, unit, D), BF),
+            ((n_t, unit, D), BF), ((tp, unit, feat), BF), ((tp, unit, feat), BF),
         ] + [((n_t,), None)] * 4, 10**10,
         tokens, mixall, wo, wb, gf, cotangent,
     )
-    dq, dkv, out_rows, gfin = call(
+    dq, dkv, out_rows, gfin, gmlall = call(
         functools.partial(back_kernel, dp, tp), 4,
-        [((3, T, 128), BF), ((3, T, 128), BF), ((unit, D), BF), ((4, part, hidden), BF)],
+        [((3, T, 128), BF), ((3, T, 128), BF), ((unit, D), BF), ((3, part, hidden), BF), ((tp, unit, D), BF)],
         [
             ((3, 8, T), F32), ((3, HEAD, T), F32), ((4, 3, T, 128), BF), ((3, 3, T, 128), BF),
             ((n_dc, part, hidden), BF), ((n_t, unit, D), BF),
-        ] + [((3,), None)] * 2 + [((n_dc,), None)] * 2 + [((3,), None)] * 2 + [((n_t,), None)] * 2,
+        ] + [((3,), None)] * 2 + [((n_dc,), None)] * 2 + [((3,), None)] * 2 + [((n_t,), None)] * 4,
         10**10,
-        q, g128, kvall, mixf, lse, outp, mid_rows, gall.reshape(4, dp, part, hidden), tab,
+        q, g128, kvall, mixf, lse, outp, mid_rows, gall.reshape(3, dp, part, hidden), tab, gml,
     )
     in_rows, gqkv, gains = call(
         functools.partial(tail_kernel, dp, tp), 5,
-        [((unit, D), BF), ((3, part, feat), BF), ((8, D), F32)],
+        [((unit, D), BF), ((4, part, feat), BF), ((8, D), F32)],
         [
-            ((D, 384), BF), ((tp, unit, D), BF), ((n_t, unit, D), BF), ((3, dp, part, feat), BF),
+            ((D, 384), BF), ((tp, unit, D), BF), ((n_t, unit, D), BF), ((4, dp, part, feat), BF),
             ((n_dc, part, feat), BF), ((8, D), F32), ((n_t, 8, D), F32), ((n_dc, 8, D), F32),
         ] + [((n_t,), None)] * 2 + [((n_dc,), None)] * 2 + [((3,), None)] * 2
         + [((n_t,), None)] * 2 + [((n_dc,), None)] * 2, 10**10,
-        dq, dkv, n1, tokens, gm_rows, wa.reshape(D, 640), gf, gain2,
+        dq, dkv, n1, tokens, gm_rows, wa.reshape(D, 640), gf, gain2, mixall, gmlall,
     )
     own = lax.dynamic_slice_in_dim(gains[:2], lax.axis_index("dp") * part, part, 1)
     return (
@@ -627,7 +637,7 @@
         gqkv[0].astype(F32),
         gqkv[1].astype(F32),
         gqkv[2].astype(F32),
-        gfin[3][:, :feat].T.astype(F32),
+        gqkv[3].T.astype(F32),
         gfin[0].astype(F32),
         gfin[1].astype(F32),
         gfin[2].T.astype(F32),

time: 346 us -> 312 us (0.902)
  Pallas kernels: 322 us -> 291 us
    pallas_call x5, Pallas kernels: 322 us -> 291 us  [call(): pl.pallas_call(kernel, out_shape=[jax.ShapeDtypeStruct(s, t) for s, t in...]
where the time goes in v2:
time: 312 us
  Pallas kernels  291 us (93%)
  local copies, waits for them, and re-layouts  16.9 us (5%)
  other arithmetic  3.26 us (1%)
    pallas_call x5, Pallas kernels, call(): pl.pallas_call(kernel, out_shape=[jax.ShapeDtypeStruct(s, t) for s, t in...  291 us
    unnamed x40, local copies, waits for them, and re-layouts  10.3 us

profile of v2, /device:TPU:0, one launch (start us, length us, event | category | flops | bytes accessed | tf_op | source)
XLA Modules:
  0.0 311.6 jit_solution(2341432377599726006)
XLA Ops:
  0.7 0.9 fusion.1
  1.6 0.1 copy.41
  1.7 0.9 fusion
  2.7 0.1 copy.43
  2.8 0.1 copy.44
  2.9 0.1 copy.45
  3.2 0.1 copy.29
  3.4 1.1 concatenate.6.pa
  4.5 2.3 constant_dynamic-slice_fusion.tab
  6.9 0.7 maximum_maximum_fusion.gn
  7.6 22.0 %shard_map.203 = (bf16[3,1024,128]{2,1,0:T(8,128)(2,1)}, bf16[3,1024,128]{2,1,0:T(8,128)(2,1)}, bf16[2,384,640]{2,1,0:T(8,128)(2,1)}, f32[16,768]{1,0:T(8,128)}, bf16[1024,768]{1,0:T(8,128)(2,1)}) custom-call(bf16[1024,768]{1,0:T(8,128)(2,1)} %tok.5, bf16[384,640]{1,0:T(8,128)(2,1)} %concatenate.6.pa, bf16[16,384]{1,0:T(8,128)(2,1)} %maximum_maximum_fusion.gn, ...), custom_call_target="tpu_custom_call" | custom-call | flops 1000000000 | bytes 10000000 | tf_op jit(solution)/shard_map/pallas_call | solution.py:540
  29.6 0.2 copy.30
  29.8 0.2 copy.31
  30.0 0.2 copy.32
  30.3 1.1 pad_maximum_fusion.pb
  31.4 0.8 copy.33
  32.2 75.6 %shard_map.204 = (bf16[4,3,1024,128]{3,2,1,0:T(8,128)(2,1)}, bf16[4,3,64,1024]{3,2,1,0:T(8,128)(2,1)}, f32[3,64,1024]{2,1,0:T(8,128)}, f32[3,8,1024]{2,1,0:T(8,1...) custom-call(bf16[3,1024,128]{2,1,0:T(8,128)(2,1)} %get-tuple-element.37.q, ...), custom_call_target="tpu_custom_call" | custom-call | flops 10000000000 | bytes 10000000 | tf_op jit(solution)/shard_map/pallas_call | solution.py:540
  107.8 59.1 %shard_map.205 = (bf16[4,256,768]{2,1,0:T(8,128)(2,1)}, f32[256,768]{1,0:T(8,128)}, f32[256,768]{1,0:T(8,128)}, bf16[3,1024,128]{2,1,0:T(8,128)(2,1)}, bf16[3,76...) custom-call(bf16[1024,768]{1,0:T(8,128)(2,1)} %tok.5, ...), custom_call_target="tpu_custom_call" | custom-call | flops 10000000000 | bytes 10000000 | tf_op jit(solution)/shard_map/pallas_call | solution.py:540
  167.0 72.7 %shard_map.206 = (bf16[3,1024,128]{2,1,0:T(8,128)(2,1)}, bf16[3,1024,128]{2,1,0:T(8,128)(2,1)}, bf16[256,768]{1,0:T(8,128)(2,1)}, bf16[3,384,288]{2,1,0:T(8,128)(2,1)}, bf16[4,256,768]{2,1,0:T(8,128)(2,1)}) custom-call(bf16[3,1024,128]{2,1,0:T(8,128)(2,1)} %get-tuple-element.37.q, bf16[3,1024,128]{2,1,0:T(8,128)(2,1)} %get-tuple-element.43.g, ...), custom_call_target="tpu_custom_call" | custom-call | flops 10000000000 | bytes 10000000 | tf_op jit(solution)/shard_map/pallas_call | solution.py:540
  239.6 61.2 %shard_map.207 = (bf16[256,768]{1,0:T(8,128)(2,1)}, bf16[4,384,192]{2,1,0:T(8,128)(2,1)}, f32[8,768]{1,0:T(8,128)}) custom-call(bf16[3,1024,128]{2,1,0:T(8,128)(2,1)} %get-tuple-element.52.dq, bf16[3,1024,128]{2,1,0:T(8,128)(2,1)} %get-tuple-element.53.dkv, bf16[1024,768]{1,0:T(8,128)(2,1)} %get-tuple-element.54.n1, bf16[1024,768]{1,0:T(8,128)(2,1)} %tok.5, ...), custom_call_target="tpu_custom_call" | custom-call | flops 10000000000 | bytes 10000000 | tf_op jit(solution)/shard_map/pallas_call | solution.py:540
  300.8 1.4 convert_bitcast_fusion.1
  302.2 0.9 copy.34
  303.1 0.9 copy.35
  303.9 0.9 copy.36
  304.8 0.9 copy.37
  305.8 1.0 copy.38
  306.8 1.0 copy.39
  307.7 1.0 copy.40
  308.7 0.7 slice.61
  309.5 0.7 dynamic-slice_reduce_fusion
  310.1 0.7 copy.49
  310.9 0.7 copy.50
  (28 shorter events, 0.5 us)
Async XLA Ops:
  0.6 2.5 copy-start.6
  3.4 3.4 %copy-start.8 = (bf16[384]{0:T(512)(128)(2,1)S(1)}, bf16[384]{0:T(512)(128)(2,1)}, u32[]{:S(2)}) copy-start(bf16[384]{0:T(512)(128)(2,1)} %param.20) | copy-start | bytes 2308
  3.4 3.4 %copy-start.9 = (bf16[384]{0:T(512)(128)(2,1)S(1)}, bf16[384]{0:T(512)(128)(2,1)}, u32[]{:S(2)}) copy-start(bf16[384]{0:T(512)(128)(2,1)} %param.21) | copy-start | bytes 2308
  7.5 22.0 %copy-start.3 = (bf16[384,288]{0,1:T(8,128)(2,1)S(1)}, bf16[384,288]{0,1:T(8,128)(2,1)}, u32[]{:S(2)}) copy-start(bf16[384,288]{0,1:T(8,128)(2,1)} %param.17) | copy-start | bytes 663556
  7.5 22.3 %copy-start.4 = (bf16[384,288]{0,1:T(8,128)(2,1)S(1)}, bf16[384,288]{0,1:T(8,128)(2,1)}, u32[]{:S(2)}) copy-start(bf16[384,288]{0,1:T(8,128)(2,1)} %param.18) | copy-start | bytes 663556
  7.6 22.5 %copy-start.5 = (bf16[288,384]{1,0:T(8,128)(2,1)S(1)}, bf16[288,384]{1,0:T(8,128)(2,1)}, u32[]{:S(2)}) copy-start(bf16[288,384]{1,0:T(8,128)(2,1)} %param.19) | copy-start | bytes 663556
  29.6 1.8 copy-start.7
  302.2 3.5 %copy-start = (bf16[3,384,288]{2,1,0:T(8,128)(2,1)S(1)}, bf16[3,384,288]{2,1,0:T(8,128)(2,1)}, u32[]{:S(2)}) copy-start(bf16[3,384,288]{2,1,0:T(8,128)(2,1)} %get-tuple-element.61) | copy-start | bytes 1990660
  305.8 4.3 %copy-start.1 = (bf16[256,768]{1,0:T(8,128)(2,1)S(1)}, bf16[256,768]{1,0:T(8,128)(2,1)}, u32[]{:S(2)}) copy-start(bf16[256,768]{1,0:T(8,128)(2,1)} %get-tuple-element.100) | copy-start | bytes 1179652
  306.8 4.1 %copy-start.2 = (bf16[256,768]{1,0:T(8,128)(2,1)S(1)}, bf16[256,768]{1,0:T(8,128)(2,1)}, u32[]{:S(2)}) copy-start(bf16[256,768]{1,0:T(8,128)(2,1)} %get-tuple-element.101) | copy-start | bytes 1179652
